TPU v7x, 128 devices: a whole 4x4x4 slice. The times are simulated.
128 devices in a mesh: ax: 8 (over y, z_lo), ay: 16 (over z_hi, x, core).
Axes of the slice: x: 4, y: 4, z: 4 (z_hi: 2, z_lo: 2; z = z_hi * 2 + z_lo), core: 2. Of those that a mesh axis runs over, the one named last changes fastest.
Arguments:
- noise: float32 [16, 2048, 4096], P(None, ('ax', 'ay')), may hold values from -6 to 6
- kappa: float32 [16, 2048, 4096], P(None, 'ax', 'ay'), may hold values from 0.05 to 2
- mask: int32 [2048, 4096], P('ax', 'ay'), may hold values 0 or 1
Outputs:
- sample: float32 [16, 2048, 4096], P(None, 'ax', 'ay')
All inputs are finite; a program needn't handle non-finite values. No bound on the sum of `mask` on one device may be relied on, other than what follows from the above.
Results may differ from a plain program's by a relative error of at most 0.00002.
Values sent between devices are 32-bit elements; how exact they have to be, the bound alone decides.
A program may use at most 128 MiB of HBM per device.

v0:
```python
import jax
import jax.numpy as jnp
from jax import lax
from jax.sharding import PartitionSpec as P


def extended(cells, sides, width):
    for axis, dim in sides:
        count = lax.axis_size(axis)
        ends = count - 1
        head = lax.slice_in_dim(cells, 0, width, axis=dim)
        tail = lax.slice_in_dim(cells, cells.shape[dim] - width, cells.shape[dim], axis=dim)
        cells = jnp.concatenate(
            [
                lax.ppermute(tail, axis, [(i, (i + 1) % count) for i in range(ends)]),
                cells,
                lax.ppermute(head, axis, [((i + 1) % count, i) for i in range(ends)]),
            ],
            axis=dim,
        )
    return cells


def neighbours(padded):
    centre = padded[:, 1:-1, 1:-1]
    with_ends = jnp.pad(centre, ((1, 1), (0, 0), (0, 0)))
    total = padded[:, 2:, 1:-1] + padded[:, :-2, 1:-1]
    total = total + padded[:, 1:-1, 2:] + padded[:, 1:-1, :-2]
    return total + with_ends[2:] + with_ends[:-2]


def factors(kappa):
    pivots = []
    for layer_index in range(kappa.shape[0]):
        diagonal = 2.5 + kappa[layer_index]
        if layer_index > 0:
            diagonal = diagonal - pivots[-1]
        pivots.append(1.0 / diagonal)
    return pivots


def thomas(field, pivots):
    layers = field.shape[0]
    forward = []
    for layer_index in range(layers):
        current = field[layer_index]
        if layer_index > 0:
            current = current + forward[-1]
        forward.append(current * pivots[layer_index])
    result = [None] * layers
    solved = forward[layers - 1]
    result[layers - 1] = solved
    for layer_index in range(layers - 2, -1, -1):
        solved = forward[layer_index] + pivots[layer_index] * solved
        result[layer_index] = solved
    return jnp.stack(result, 0)


def body(noise, kappa, mask):
    layers = kappa.shape[0]
    stacked = jnp.concatenate([kappa, mask[None].astype(jnp.float32)], 0)
    strip_coef = lax.all_to_all(stacked, "ay", split_axis=1, concat_axis=2, tiled=True)
    strip_kappa = strip_coef[:layers]
    strip_mask = strip_coef[layers:]
    inverse = strip_mask / (6.0 + strip_kappa)
    pivots = factors(strip_kappa)
    field = inverse * noise
    for repeat in range(2):
        padded = extended(field, ((("ax", "ay"), 1),), 1)
        padded = jnp.pad(padded, ((0, 0), (0, 0), (1, 1)))
        field = inverse * (noise + neighbours(padded))
    strip_sample = thomas(field, pivots)
    return lax.all_to_all(strip_sample, "ay", split_axis=2, concat_axis=1, tiled=True)


def solution(mesh):
    in_specs = (P(None, ("ax", "ay"), None), P(None, "ax", "ay"), P("ax", "ay"))
    out_specs = P(None, "ax", "ay")
    return jax.shard_map(body, mesh=mesh, in_specs=in_specs, out_specs=out_specs, check_vma=False)
```

profile of v0, /device:TPU:1, one launch (start us, length us, event | category | flops | bytes accessed | tf_op | source)
XLA Modules:
  0.0 360.2 jit_solution(16229314087729215411)
XLA Ops:
  0.0 4.7 %copy.32 = f32[16,256,256]{2,0,1:T(8,128)S(1)} copy(f32[16,256,256]{2,1,0:T(8,128)} %param.4) | data formatting | bytes 8388608 | tf_op args[1]
  4.7 0.3 copy.33
  5.0 0.6 pad_maximum_fusion
  5.6 82.1 %all_to_all.33 = f32[17,256,256]{2,0,1:T(8,128)S(1)} all-to-all(f32[17,256,256]{2,0,1:T(8,128)S(1)} %pad_maximum_fusion), channel_id=1, replica_groups=mesh['ax'=8,'ay'=16] {'ay'}, dimensions={1} | all-to-all | bytes 8912896 | tf_op jit(solution)/shard_map/all_to_all | solution.py:62
  87.7 2.6 copy.51
  90.3 1.8 slice_add_fusion.31
  92.1 2.5 slice_add_fusion.4
  94.6 0.2 copy.49
  94.8 5.0 %add.1311 = f32[16,16,4096]{2,1,0:T(8,128)} reshape(f32[16,16,16,256]{3,2,1,0:T(8,128)} %slice_add_fusion.4) | data formatting | bytes 8388608 | tf_op jit(solution)/shard_map/add | solution.py:65
  99.8 4.5 %fusion.34 = f32[16,16,4096]{2,1,0:T(8,128)S(1)} fusion(f32[16,16,4096]{2,1,0:T(8,128)} %param.3, f32[16,16,4096]{2,1,0:T(8,128)} %add.1311, f32[16,4096]{1,0:T(8,128)S(1)} %bitcast.54), kind=kLoop, calls=%fused_computation.126 | loop fusion | flops 2097152 | bytes 12845056 | tf_op jit(solution)/shard_map/mul | solution.py:67
  104.3 0.4 fusion.44
  104.7 0.2 copy.35
  104.9 3.0 collective-permute-start
  107.8 0.2 copy.37
  108.0 2.8 collective-permute-start.1
  110.8 1.8 collective-permute-done
  112.5 0.3 copy.36
  112.8 1.1 collective-permute-done.1
  113.9 0.3 copy.38
  114.2 5.2 %select_maximum_fusion.2 = f32[16,18,4098]{2,1,0:T(8,128)} fusion(f32[16,1,4096]{2,1,0:T(1,128)S(1)} %copy.36, f32[16,16,4096]{2,1,0:T(8,128)S(1)} %fusion.34, f32[16,1,4096]{2,1,0:T(1,128)S(1)} %copy.38), kind=kLoop, calls=%fused_computation.4 | loop fusion | flops 9441792 | bytes 9439488 | tf_op jit(solution)/shard_map/concatenate | solution.py:13
  119.4 13.9 %fusion.4 = f32[16,16,4096]{2,1,0:T(8,128)S(1)} fusion(f32[16,16,4096]{2,1,0:T(8,128)} %param.3, f32[16,16,4096]{2,1,0:T(8,128)} %copy-done.4, f32[16,18,4098]{2,1,0:T(8,128)} %select_maximum_fusion.2, f32[16,1,4096]{2,1,0:T(1,128)S(1)} %copy.38, f32[16,1,4096]{2,1,0:T(1,128)S(1)} %copy.36, f32[16,16,4096]{2,1,0:T(8,128)S(1)} %copy-done, ...), kind=kLoop, calls=%fused_computation.16 | loop fusion | flops 10485760 | bytes 25952256 | tf_op jit(solution)/shard_map/mul | solution.py:71
  133.3 2.0 copy-done.2
  135.3 0.4 fusion.43
  135.8 0.9 copy.41
  136.6 1.9 collective-permute-start.2
  138.5 0.8 copy.43
  139.4 4.6 %collective-permute-start.3 = (f32[16,1,4096]{2,0,1:T(8,128)}, f32[16,1,4096]{2,0,1:T(8,128)}, u32[]{:S(2)}, u32[]{:S(2)}) collective-permute-start(f32[16,1,4096]{2,0,1:T(8,128)} %copy.43), channel_id=1, source_target_pairs={{0,1},{1,2},{2,3},{3,4},{4,5},{5,6},{6,7},{7,8},{8,9},{9,10},{10,1... | collective-permute-start | bytes 786440 | tf_op jit(solution)/shard_map/ppermute | solution.py:15
  144.0 1.0 add.1363
  145.4 1.0 add.1342
  146.4 1.7 add.1345
  148.1 1.7 add.1348
  149.8 1.7 add.1351
  151.5 1.7 add.1354
  153.2 1.7 add.1357
  154.9 0.8 add.1360
  155.6 0.8 add.1369
  156.4 0.8 div.777
  157.2 1.2 copy.42
  158.4 1.2 copy.44
  159.6 7.0 %select_maximum_fusion = f32[16,18,4098]{2,1,0:T(8,128)} fusion(f32[16,1,4096]{2,1,0:T(1,128)S(1)} %copy.42, f32[16,16,4096]{2,1,0:T(8,128)} %copy-done.2, f32[16,1,4096]{2,1,0:T(1,128)S(1)} %copy.44), kind=kLoop, calls=%fused_computation.2 | loop fusion | flops 9441792 | bytes 9439488 | tf_op jit(solution)/shard_map/concatenate | solution.py:13
  166.6 9.5 %fusion.8 = f32[16,16,4096]{2,1,0:T(8,128)} fusion(f32[16,16,4096]{2,1,0:T(8,128)} %param.3, f32[16,16,4096]{2,1,0:T(8,128)S(1)} %copy-done.3, f32[16,18,4098]{2,1,0:T(8,128)} %select_maximum_fusion, f32[16,1,4096]{2,1,0:T(1,128)S(1)} %copy.44, f32[16,1,4096]{2,1,0:T(1,128)S(1)} %copy.42, f32[16,16,4096]{2,1,0:T(8,128)S(1)} %copy-done.1, ...), kind=kLoop, calls=%fused_computation.20 | loop fusion | flops 10485760 | bytes 25952256 | tf_op jit(solution)/shard_map/mul | solution.py:71
  176.1 4.6 %add_dynamic-update-slice_fusion = (f32[16,16,4096]{2,1,0:T(8,128)}, f32[1,16,4096]{2,1,0:T(8,128)S(1)}, f32[1,16,4096]{2,1,0:T(8,128)S(1)}, f32[1,16,4096]{2,1,...) fusion(f32[1,16,4096]{2,1,0:T(8,128)} %div.777, ...), kind=kLoop, calls=%fused_computation.81 | loop fusion | flops 5963775 | bytes 14155776
  180.7 0.7 constant_dynamic-update-slice_fusion.7
  181.4 1.7 fusion.33
  183.1 0.7 constant_dynamic-update-slice_fusion.6
  183.9 1.7 fusion.32
  185.6 0.7 constant_dynamic-update-slice_fusion.5
  186.3 1.7 fusion.31
  188.1 0.7 constant_dynamic-update-slice_fusion.4
  188.8 1.7 fusion.30
  190.5 0.7 constant_dynamic-update-slice_fusion.3
  191.3 1.7 fusion.29
  193.0 0.7 constant_dynamic-update-slice_fusion.2
  193.7 1.7 fusion.28
  195.4 0.8 constant_dynamic-update-slice_fusion.1
  196.2 1.8 fusion.27
  198.0 0.7 constant_dynamic-update-slice_fusion
  198.7 18.0 %copy.47 = f32[16,16,4096]{1,0,2:T(8,128)} copy(f32[16,16,4096]{2,1,0:T(8,128)} %constant_dynamic-update-slice_fusion) | data formatting | bytes 8388608 | tf_op jit(solution)/shard_map/stack | solution.py:56
  216.7 22.0 %reshape.925 = f32[16,1,65536]{2,1,0:T(1,128)} reshape(f32[4096,16,16]{2,1,0:T(8,128)} %bitcast.49) | data formatting | bytes 8388608
  238.6 60.9 %all_to_all.34 = f32[16,1,65536]{2,1,0:T(1,128)} all-to-all(f32[16,1,65536]{2,1,0:T(1,128)} %reshape.925), channel_id=1, replica_groups=mesh['ax'=8,'ay'=16] {'ay'}, dimensions={0} | all-to-all | bytes 8388608 | tf_op jit(solution)/shard_map/all_to_all | solution.py:73
  299.6 0.6 broadcast.1589
  300.1 13.8 %reduce = f32[16,65536]{1,0:T(8,128)} reduce(f32[16,1,65536]{2,1,0:T(1,128)} %all_to_all.34, f32[]{:T(128)} %broadcast.1589), dimensions={1}, to_apply=%all_to_all.27.reduce_sub_computation | reduce | bytes 8388612 | tf_op jit(solution)/shard_map/all_to_all | solution.py:73
  313.9 25.7 %reshape.926 = f32[4096,16,16]{2,1,0:T(8,128)} reshape(f32[16,65536]{1,0:T(8,128)} %reduce) | data formatting | bytes 8388608
  339.6 20.6 %copy.48 = f32[16,16,16,256]{3,2,1,0:T(8,128)} copy(f32[16,16,16,256]{2,0,3,1:T(8,128)} %bitcast.50) | data formatting | bytes 8388608 | tf_op jit(solution)/shard_map/all_to_all | solution.py:73
  (22 shorter events, 0.4 us)
Async XLA Ops:
  0.0 4.7 %copy-start.6 = (s32[256,256]{1,0:T(8,128)S(1)}, s32[256,256]{1,0:T(8,128)}, u32[]{:S(2)}) copy-start(s32[256,256]{1,0:T(8,128)} %param.5) | copy-start | bytes 786436
  104.3 9.9 %copy-start.4 = (f32[16,16,4096]{2,1,0:T(8,128)}, f32[16,16,4096]{2,1,0:T(8,128)S(1)}, u32[]{:S(2)}) copy-start(f32[16,16,4096]{2,1,0:T(8,128)S(1)} %fusion.34) | copy-start | bytes 12582916
  104.9 7.7 %collective-permute-start = (f32[16,1,4096]{2,0,1:T(8,128)S(1)}, f32[16,1,4096]{2,0,1:T(8,128)S(1)}, u32[]{:S(2)}, u32[]{:S(2)}) collective-permute-start(f32[16,1,4096]{2,0,1:T(8,128)S(1)} %copy.35), channel_id=1, source_target_pairs={{1,0},{2,1},{3,2},{4,3},{5,4},{6,5},{7,6},{8,7},{9,8},{10,9},{11,1... | collective-permute-start | bytes 786440 | tf_op jit(solution)/shard_map/ppermute | solution.py:17
  108.0 5.9 %collective-permute-start.1 = (f32[16,1,4096]{2,0,1:T(8,128)S(1)}, f32[16,1,4096]{2,0,1:T(8,128)S(1)}, u32[]{:S(2)}, u32[]{:S(2)}) collective-permute-start(f32[16,1,4096]{2,0,1:T(8,128)S(1)} %copy.37), channel_id=1, source_target_pairs={{0,1},{1,2},{2,3},{3,4},{4,5},{5,6},{6,7},{7,8},{8,9},{9,10},{10,1... | collective-permute-start | bytes 786440 | tf_op jit(solution)/shard_map/ppermute | solution.py:15
  114.2 5.3 %copy-start = (f32[16,16,4096]{2,1,0:T(8,128)S(1)}, f32[16,16,4096]{2,1,0:T(8,128)}, u32[]{:S(2)}) copy-start(f32[16,16,4096]{2,1,0:T(8,128)} %add.1311) | copy-start | bytes 12582916
  133.3 2.0 copy-start.2
  135.7 19.1 %copy-start.5 = (f32[1,16,16,256]{3,2,1,0:T(8,128)S(1)}, f32[1,16,16,256]{3,2,1,0:T(8,128)}, u32[]{:S(2)}) copy-start(f32[1,16,16,256]{3,2,1,0:T(8,128)} %get-tuple-element.31) | copy-start | bytes 786436
  136.6 20.5 %collective-permute-start.2 = (f32[16,1,4096]{2,0,1:T(8,128)}, f32[16,1,4096]{2,0,1:T(8,128)}, u32[]{:S(2)}, u32[]{:S(2)}) collective-permute-start(f32[16,1,4096]{2,0,1:T(8,128)} %copy.41), channel_id=1, source_target_pairs={{1,0},{2,1},{3,2},{4,3},{5,4},{6,5},{7,6},{8,7},{9,8},{10,9},{11,1... | collective-permute-start | bytes 786440 | tf_op jit(solution)/shard_map/ppermute | solution.py:17
  139.4 19.0 %collective-permute-start.3 = (f32[16,1,4096]{2,0,1:T(8,128)}, f32[16,1,4096]{2,0,1:T(8,128)}, u32[]{:S(2)}, u32[]{:S(2)}) collective-permute-start(f32[16,1,4096]{2,0,1:T(8,128)} %copy.43), channel_id=1, source_target_pairs={{0,1},{1,2},{2,3},{3,4},{4,5},{5,6},{6,7},{7,8},{8,9},{9,10},{10,1... | collective-permute-start | bytes 786440 | tf_op jit(solution)/shard_map/ppermute | solution.py:15
  159.6 7.0 %copy-start.1 = (f32[16,16,4096]{2,1,0:T(8,128)S(1)}, f32[16,16,4096]{2,1,0:T(8,128)}, u32[]{:S(2)}) copy-start(f32[16,16,4096]{2,1,0:T(8,128)} %add.1311) | copy-start | bytes 12582916
  159.6 7.0 %copy-start.3 = (f32[16,16,4096]{2,1,0:T(8,128)S(1)}, f32[16,16,4096]{2,1,0:T(8,128)}, u32[]{:S(2)}) copy-start(f32[16,16,4096]{2,1,0:T(8,128)} %copy-done.2) | copy-start | bytes 12582916
where the time goes:
time: 362 us; the launch traced here: 360 us
  blocking collectives  143 us (40%)
  local copies, waits for them, and re-layouts  126 us (35%)
  other arithmetic  75.5 us (21%)
  starting transfers between devices  12.3 us (3%)
    all_to_all x1, blocking collectives, body(): lax.all_to_all(stacked, 'ay', split_axis=1, concat_axis=2, tiled=True)  82.1 us
    all_to_all x1, blocking collectives, body(): lax.all_to_all(strip_sample, 'ay', split_axis=2, concat_axis=1, tiled=True)  60.9 us
    unnamed x25, local copies, waits for them, and re-layouts  59.6 us
    mul x2, other arithmetic, body(): field = inverse * (noise + neighbours(padded))  23.4 us
    all_to_all x2, local copies, waits for them, and re-layouts, body(): lax.all_to_all(strip_sample, 'ay', split_axis=2, concat_axis=1, tiled=True)  21.1 us
    another operation x2, local copies, waits for them, and re-layouts, thomas(): return jnp.stack(result, 0)  18.7 us
    unnamed x8, other arithmetic  16.8 us
    all_to_all x1, other arithmetic, body(): lax.all_to_all(strip_sample, 'ay', split_axis=2, concat_axis=1, tiled=True)  13.8 us
  transfers between devices with their start and end apart: 4, of which 2 were waited for; matrix products, arithmetic and copies ran while one was open for 4% of the time, Pallas kernels for 0%

commit v1 on v0

v1 whole, which is shorter than its diff:
```python
import functools

import jax
import jax.numpy as jnp
from jax import lax
from jax.experimental import pallas as pl
from jax.experimental.pallas import tpu as pltpu
from jax.sharding import PartitionSpec as P

MESH = pl.DeviceIdType.MESH
F32 = jnp.float32
NL = 16
SR = 16
BC = 256
TOP = 16
EARLY = 4


def wait_bytes(ref, sem):
    pltpu.make_async_copy(ref, ref, sem).wait()


def kernel(na, nd, noise, kappa, mask, out, *scratch):
    (strip, kap, msk, noise_x, inv_x, init_x, mid_x, fwd, rows_send, rowi_send, rown, rowi, q_send, qn, qi, qp,
     e_send, e_recv, load_sem, bulk_send, bulk_recv, q_ssem, q_rsem, r_ssem, r_rsem, qh_ssem, qh_rsem,
     e_ssem, e_rsem, i_ssem, i_rsem, c_ssem, c_rsem, out_sem) = scratch
    br = nd * SR
    end = TOP + br
    a, d = lax.axis_index("ax"), lax.axis_index("ay")
    above, below = lax.rem(a + na - 1, na), lax.rem(a + 1, na)
    left, right = lax.rem(d + nd - 1, nd), lax.rem(d + 1, nd)

    loads = [
        pltpu.make_async_copy(noise, strip, load_sem.at[0]),
        pltpu.make_async_copy(kappa, kap, load_sem.at[1]),
        pltpu.make_async_copy(mask, msk, load_sem.at[2]),
    ]
    for load in loads:
        load.start()

    barrier = pltpu.get_barrier_semaphore()

    def greet(x, y):
        pl.semaphore_signal(barrier, inc=1, device_id=(x, y), device_id_type=MESH)

    @pl.loop(1, nd)
    def _(k):
        greet(a, lax.rem(d + k, nd))

    for x in (above, below):
        for y in (d, left, right):
            greet(x, y)
    greet(above, nd - 1)
    greet(below, 0)
    edge = jnp.where(d == 0, nd, 0) + jnp.where(d == nd - 1, nd, 0)
    pl.semaphore_wait(barrier, nd - 1 + 6 + edge)

    def bulk(layer):
        pltpu.make_async_copy(
            noise.at[layer, :, pl.ds(pl.multiple_of(d * BC, BC), BC)],
            noise_x.at[layer, pl.ds(pl.multiple_of(TOP + d * SR, SR), SR), :],
            bulk_recv.at[layer],
        ).start()

        @pl.loop(1, nd)
        def _(k):
            t = lax.rem(d + k, nd)
            pltpu.make_async_remote_copy(
                src_ref=noise.at[layer, :, pl.ds(pl.multiple_of(t * BC, BC), BC)],
                dst_ref=noise_x.at[layer, pl.ds(pl.multiple_of(TOP + d * SR, SR), SR), :],
                send_sem=bulk_send.at[layer],
                recv_sem=bulk_recv.at[layer],
                device_id=(a, t),
                device_id_type=MESH,
            ).start()

    @pl.loop(0, EARLY)
    def _(layer):
        bulk(layer)

    lane = lax.broadcasted_iota(jnp.int32, (SR, 128), 1)
    sub = lax.broadcasted_iota(jnp.int32, (8, BC), 0)

    loads[0].wait()

    @pl.loop(0, nd)
    def _(t):
        before = pl.multiple_of(lax.rem(t + nd - 1, nd) * BC + 128, 128)
        after = pl.multiple_of(lax.rem(t + 1, nd) * BC, 128)
        packed = jnp.zeros((SR, 128), F32)
        for layer in range(NL):
            both = jnp.where(lane < 64, strip[layer, :, pl.ds(after, 128)], strip[layer, :, pl.ds(before, 128)])
            packed = jnp.where(lane // 4 == layer, pltpu.roll(both, (4 * layer + 2) % 128, 1), packed)
        q_send[t] = packed

    def q_place(s):
        return qn.at[pl.ds(pl.multiple_of(TOP + s * SR, SR), SR), :]

    pltpu.make_async_copy(q_send.at[d], q_place(d), q_rsem).start()

    @pl.loop(1, nd)
    def _(k):
        t = lax.rem(d + k, nd)
        pltpu.make_async_remote_copy(
            src_ref=q_send.at[t], dst_ref=q_place(d), send_sem=q_ssem, recv_sem=q_rsem,
            device_id=(a, t), device_id_type=MESH,
        ).start()

    def pick_rows(tile, first, i):
        return pltpu.roll(tile, (2 * i - first) % 8, 0)

    def send_rows(first_row, first, x, slot, q_src, q_dst):
        @pl.loop(0, nd)
        def _(t):
            cols = pl.ds(pl.multiple_of(t * BC, BC), BC)
            for q in range(NL // 4):
                packed = jnp.zeros((8, BC), F32)
                for i in range(4):
                    tile = strip[4 * q + i, first_row:first_row + 8, cols]
                    packed = jnp.where(sub // 2 == i, pick_rows(tile, first, i), packed)
                rows_send[q, :, cols] = packed
            pltpu.make_async_remote_copy(
                src_ref=rows_send.at[:, :, cols], dst_ref=rown.at[slot], send_sem=r_ssem, recv_sem=r_rsem.at[slot],
                device_id=(x, t), device_id_type=MESH,
            ).start()
            pltpu.make_async_remote_copy(
                src_ref=q_send.at[t, q_src:q_src + 8, :], dst_ref=qn.at[q_dst:q_dst + 8, :], send_sem=qh_ssem,
                recv_sem=qh_rsem.at[slot], device_id=(x, t), device_id_type=MESH,
            ).start()

    @pl.when(d == 0)
    def _():
        send_rows(0, 0, above, 1, 0, end)

    @pl.when(d == nd - 1)
    def _():
        send_rows(SR - 8, 6, below, 0, SR - 8, TOP - 8)

    loads[1].wait()
    loads[2].wait()
    rb = 32
    lane_b = lax.broadcasted_iota(jnp.int32, (rb, 128), 1)

    @pl.loop(0, br // rb)
    def _(b):
        rows = pl.ds(pl.multiple_of(b * rb, rb), rb)
        active = msk[rows, :].astype(F32)
        packed = jnp.zeros((rb, 128), F32)
        for layer in range(NL):
            inverse = active / (6.0 + kap[layer, rows, :])
            inv_x[layer, pl.ds(pl.multiple_of(TOP + b * rb, 16), rb), :] = inverse
            both = jnp.where(lane_b < 64, inverse[:, :128], inverse[:, 128:])
            packed = jnp.where(lane_b // 4 == layer, pltpu.roll(both, (4 * layer + 2) % 128, 1), packed)
        e_send[rows, :] = packed

    halos = []
    for slot, y in ((0, right), (1, left)):
        halos.append(pltpu.make_async_remote_copy(
            src_ref=e_send, dst_ref=e_recv.at[slot, TOP:end, :], send_sem=e_ssem.at[slot], recv_sem=e_rsem.at[slot],
            device_id=(a, y), device_id_type=MESH,
        ))
        halos.append(pltpu.make_async_remote_copy(
            src_ref=e_send.at[br - 8:br, :], dst_ref=e_recv.at[slot, TOP - 8:TOP, :], send_sem=c_ssem.at[slot, 0],
            recv_sem=c_rsem.at[slot, 0], device_id=(below, y), device_id_type=MESH,
        ))
        halos.append(pltpu.make_async_remote_copy(
            src_ref=e_send.at[0:8, :], dst_ref=e_recv.at[slot, end:end + 8, :], send_sem=c_ssem.at[slot, 1],
            recv_sem=c_rsem.at[slot, 1], device_id=(above, y), device_id_type=MESH,
        ))
    for q in range(NL // 4):
        down = jnp.zeros((8, BC), F32)
        up = jnp.zeros((8, BC), F32)
        for i in range(4):
            layer = 4 * q + i
            down = jnp.where(sub // 2 == i, pick_rows(inv_x[layer, end - 8:end, :], 6, i), down)
            up = jnp.where(sub // 2 == i, pick_rows(inv_x[layer, TOP:TOP + 8, :], 0, i), up)
        rowi_send[0, q] = down
        rowi_send[1, q] = up
    for slot, x in ((0, below), (1, above)):
        halos.append(pltpu.make_async_remote_copy(
            src_ref=rowi_send.at[slot], dst_ref=rowi.at[slot], send_sem=i_ssem.at[slot], recv_sem=i_rsem.at[slot],
            device_id=(x, d), device_id_type=MESH,
        ))
    for halo in halos:
        halo.start()

    @pl.loop(EARLY, NL)
    def _(layer):
        bulk(layer)

    @pl.loop(0, br // rb)
    def _(b):
        rows = pl.ds(pl.multiple_of(b * rb, rb), rb)
        pivot = jnp.zeros((rb, BC), F32)
        for layer in range(NL):
            pivot = 1.0 / (2.5 + kap[layer, rows, :] - pivot)
            kap[layer, rows, :] = pivot

    @pl.loop(0, (br + 16) // 16)
    def _(b):
        rows = pl.ds(pl.multiple_of(8 + b * 16, 8), 16)
        for field in (init_x, mid_x):
            for layer in (0, NL + 1):
                field[layer, rows, :] = jnp.zeros((16, BC + 128), F32)

    @pl.loop(0, br // 16)
    def _(b):
        fwd[0, pl.ds(pl.multiple_of(b * 16, 16), 16), :] = jnp.zeros((16, BC), F32)

    for halo in halos:
        halo.wait()
    for slot in range(2):
        wait_bytes(rown.at[slot], r_rsem.at[slot])
        place = (TOP - 8, end)[slot]
        wait_bytes(qn.at[place:place + 8, :], qh_rsem.at[slot])
    wait_bytes(qn.at[TOP:end, :], q_rsem)
    keep_top = jnp.where(a > 0, 1.0, 0.0).astype(F32)
    keep_end = jnp.where(a < na - 1, 1.0, 0.0).astype(F32)
    keep_left = jnp.where(d > 0, 1.0, 0.0).astype(F32)
    keep_right = jnp.where(d < nd - 1, 1.0, 0.0).astype(F32)

    @pl.loop(0, NL // 4)
    def _(q):
        for i in range(4):
            layer = 4 * q + i
            inv_x[layer, TOP - 8:TOP, :] = keep_top * pltpu.roll(rowi[0, q], (6 - 2 * i) % 8, 0)
            inv_x[layer, end:end + 8, :] = keep_end * pltpu.roll(rowi[1, q], (-2 * i) % 8, 0)
            noise_x[layer, TOP - 8:TOP, :] = pltpu.roll(rown[0, q], (6 - 2 * i) % 8, 0)
            noise_x[layer, end:end + 8, :] = pltpu.roll(rown[1, q], (-2 * i) % 8, 0)

    lane8 = lax.broadcasted_iota(jnp.int32, (8, 128), 1)

    @pl.loop(0, (br + 16) // 8)
    def _(b):
        rows = pl.ds(pl.multiple_of(8 + b * 8, 8), 8)
        keep = jnp.where(b == 0, keep_top, jnp.where(b == (br + 16) // 8 - 1, keep_end, 1.0))
        inverse = jnp.where(lane8 % 4 < 2, e_recv[0, rows, :] * (keep * keep_left), e_recv[1, rows, :] * (keep * keep_right))
        qi[rows, :] = inverse
        qp[rows, :] = inverse * qn[rows, :]

    def sideways(field):
        return pltpu.roll(field, 1, 1) + pltpu.roll(field, BC + 127, 1)

    def around(field, layer, first):
        near = field[layer + 1, pl.ds(first - 8, 32), :]
        rows = pl.ds(first, 16)
        return near[7:23] + near[9:25] + sideways(near[8:24]) + field[layer, rows, :] + field[layer + 2, rows, :]

    def initial(layer):
        turn = lax.rem(254 - 4 * layer, 128)

        @pl.loop(0, (br + 16) // 16)
        def _(b):
            rows = pl.ds(pl.multiple_of(8 + b * 16, 8), 16)
            init_x[layer + 1, rows, :BC] = inv_x[layer, rows, :] * noise_x[layer, rows, :]
            init_x[layer + 1, rows, BC:] = pltpu.roll(qp[rows, :], turn, 1)

    def middle(layer):
        turn = lax.rem(254 - 4 * layer, 128)

        @pl.loop(0, (br + 16) // 16)
        def _(b):
            first = pl.multiple_of(8 + b * 16, 8)
            rows = pl.ds(first, 16)
            total = around(init_x, layer, first)
            mid_x[layer + 1, rows, :BC] = inv_x[layer, rows, :] * (noise_x[layer, rows, :] + total[:, :BC])
            mid_x[layer + 1, rows, BC:] = pltpu.roll(qi[rows, :], turn, 1) * (pltpu.roll(qn[rows, :], turn, 1) + total[:, BC:])

    def smooth(layer):
        @pl.loop(0, br // 16)
        def _(b):
            first = pl.multiple_of(TOP + b * 16, 16)
            rows = pl.ds(first, 16)
            own = pl.ds(pl.multiple_of(b * 16, 16), 16)
            total = around(mid_x, layer, first)[:, :BC]
            field = inv_x[layer, rows, :] * (noise_x[layer, rows, :] + total)
            fwd[layer + 1, own, :] = (field + fwd[layer, own, :]) * kap[layer, own, :]

    @pl.loop(0, NL + 2)
    def _(step):
        @pl.when(step < NL)
        def _():
            wait_bytes(noise_x.at[step, TOP:end, :], bulk_recv.at[step])
            initial(step)

        @pl.when((step >= 1) & (step <= NL))
        def _():
            middle(step - 1)

        @pl.when(step >= 2)
        def _():
            smooth(step - 2)

    def result(b):
        rows = pl.ds(pl.multiple_of(b * rb, rb), rb)
        return pltpu.make_async_copy(fwd.at[1:NL + 1, rows, :], out.at[:, rows, :], out_sem.at[b])

    @pl.loop(0, br // rb)
    def _(b):
        rows = pl.ds(pl.multiple_of(b * rb, rb), rb)
        solved = fwd[NL, rows, :]
        for layer in range(NL - 2, -1, -1):
            solved = fwd[layer + 1, rows, :] + kap[layer, rows, :] * solved
            fwd[layer + 1, rows, :] = solved
        result(b).start()

    @pl.loop(0, NL)
    def _(layer):
        wait_bytes(noise.at[layer, :, :(nd - 1) * BC], bulk_send.at[layer])

    wait_bytes(q_send.at[:nd - 1], q_ssem)

    @pl.when((d == 0) | (d == nd - 1))
    def _():
        wait_bytes(rows_send, r_ssem)
        wait_bytes(q_send.at[:, 0:8, :], qh_ssem)

    @pl.loop(0, br // rb)
    def _(b):
        result(b).wait()


def body(noise, kappa, mask):
    na, nd = lax.axis_size("ax"), lax.axis_size("ay")
    br = nd * SR
    ext = br + 2 * TOP
    dma = pltpu.SemaphoreType.DMA
    scratch = [
        pltpu.VMEM((NL, SR, nd * BC), F32),
        pltpu.VMEM((NL, br, BC), F32),
        pltpu.VMEM((br, BC), jnp.int32),
        pltpu.VMEM((NL, ext, BC), F32),
        pltpu.VMEM((NL, ext, BC), F32),
        pltpu.VMEM((NL + 2, ext, BC + 128), F32),
        pltpu.VMEM((NL + 2, ext, BC + 128), F32),
        pltpu.VMEM((NL + 1, br, BC), F32),
        pltpu.VMEM((NL // 4, 8, nd * BC), F32),
        pltpu.VMEM((2, NL // 4, 8, BC), F32),
        pltpu.VMEM((2, NL // 4, 8, BC), F32),
        pltpu.VMEM((2, NL // 4, 8, BC), F32),
        pltpu.VMEM((nd, SR, 128), F32),
        pltpu.VMEM((ext, 128), F32),
        pltpu.VMEM((ext, 128), F32),
        pltpu.VMEM((ext, 128), F32),
        pltpu.VMEM((br, 128), F32),
        pltpu.VMEM((2, ext, 128), F32),
        dma((3,)), dma((NL,)), dma((NL,)),
        dma, dma,
        dma, dma((2,)),
        dma, dma((2,)),
        dma((2,)), dma((2,)),
        dma((2,)), dma((2,)),
        dma((2, 2)), dma((2, 2)),
        dma((br // 32,)),
    ]
    return pl.pallas_call(
        functools.partial(kernel, na, nd),
        out_shape=jax.ShapeDtypeStruct((NL, br, BC), F32),
        in_specs=[pl.BlockSpec(memory_space=pl.ANY)] * 3,
        out_specs=pl.BlockSpec(memory_space=pl.ANY),
        scratch_shapes=scratch,
        compiler_params=pltpu.CompilerParams(collective_id=0, has_side_effects=True, vmem_limit_bytes=60 << 20),
        name="sweeps",
    )(noise, kappa, mask)


def solution(mesh):
    in_specs = (P(None, ("ax", "ay"), None), P(None, "ax", "ay"), P("ax", "ay"))
    out_specs = P(None, "ax", "ay")
    return jax.shard_map(body, mesh=mesh, in_specs=in_specs, out_specs=out_specs, check_vma=False)
```

time: 362 us -> 115 us (0.32)
  the two profiles are of different devices: /device:TPU:1 before, /device:TPU:24 now
where the time goes in v1:
time: 115 us
  Pallas kernels  111 us (97%)
  local copies, waits for them, and re-layouts  4.6 us (4%)
    pallas_call x1, Pallas kernels, body(): pl.pallas_call(functools.partial(kernel, na, nd), out_shape=jax.ShapeDtyp...  111 us
    unnamed x1, local copies, waits for them, and re-layouts  4.6 us

profile of v1, /device:TPU:24, one launch (start us, length us, event | category | flops | bytes accessed | tf_op | source)
XLA Modules:
  0.0 115.3 jit_solution(1990850138376009611)
XLA Ops:
  0.0 110.7 %sweeps.1 = f32[16,256,256]{2,1,0:T(8,128)} custom-call(f32[16,16,4096]{2,1,0:T(8,128)} %noise.1, f32[16,256,256]{2,1,0:T(8,128)} %kappa.1, s32[256,256]{1,0:T(8,128)} %mask.1), custom_call_target="tpu_custom_call" | custom-call | tf_op jit(solution)/shard_map/sweeps/pallas_call | solution.py:356
  110.7 4.6 %copy.5 = f32[16,256,256]{2,1,0:T(8,128)} copy(f32[16,256,256]{2,1,0:T(8,128)} %sweeps.1) | data formatting | bytes 8388608

commit v2 on v1

--- a/solution.py
+++ b/solution.py
@@ -13,6 +13,9 @@
 SR = 16
 BC = 256
 TOP = 16
+UG = 17
+US = 16
+RB = 32
 EARLY = 4
 
 
@@ -20,10 +23,10 @@
     pltpu.make_async_copy(ref, ref, sem).wait()
 
 
-def kernel(na, nd, noise, kappa, mask, out, *scratch):
-    (strip, kap, msk, noise_x, inv_x, init_x, mid_x, fwd, rows_send, rowi_send, rown, rowi, q_send, qn, qi, qp,
+def kernel(na, nd, noise, kappa, mask, fwd, kap, *scratch):
+    (strip, msk, noise_x, inv_x, init_x, mid_x, rows_send, rowi_send, rown, rowi, q_send, qn, qi, qp, h_init, h_mid,
      e_send, e_recv, load_sem, bulk_send, bulk_recv, q_ssem, q_rsem, r_ssem, r_rsem, qh_ssem, qh_rsem,
-     e_ssem, e_rsem, i_ssem, i_rsem, c_ssem, c_rsem, out_sem) = scratch
+     e_ssem, e_rsem, i_ssem, i_rsem, c_ssem, c_rsem) = scratch
     br = nd * SR
     end = TOP + br
     a, d = lax.axis_index("ax"), lax.axis_index("ay")
@@ -86,11 +89,15 @@
     @pl.loop(0, nd)
     def _(t):
         before = pl.multiple_of(lax.rem(t + nd - 1, nd) * BC + 128, 128)
+        here = pl.multiple_of(t * BC, BC)
         after = pl.multiple_of(lax.rem(t + 1, nd) * BC, 128)
         packed = jnp.zeros((SR, 128), F32)
         for layer in range(NL):
-            both = jnp.where(lane < 64, strip[layer, :, pl.ds(after, 128)], strip[layer, :, pl.ds(before, 128)])
-            packed = jnp.where(lane // 4 == layer, pltpu.roll(both, (4 * layer + 2) % 128, 1), packed)
+            low = jnp.where(lane < 64, strip[layer, :, pl.ds(here, 128)], strip[layer, :, pl.ds(before, 128)])
+            high = jnp.where(lane < 64, strip[layer, :, pl.ds(after, 128)], strip[layer, :, pl.ds(here + 128, 128)])
+            low = pltpu.roll(low, (8 * layer + 2) % 128, 1)
+            high = pltpu.roll(high, (8 * layer + 5) % 128, 1)
+            packed = jnp.where(lane // 8 == layer, jnp.where(lane % 8 < 4, low, high), packed)
         q_send[t] = packed
 
     def q_place(s):
@@ -150,7 +157,9 @@
             inverse = active / (6.0 + kap[layer, rows, :])
             inv_x[layer, pl.ds(pl.multiple_of(TOP + b * rb, 16), rb), :] = inverse
             both = jnp.where(lane_b < 64, inverse[:, :128], inverse[:, 128:])
-            packed = jnp.where(lane_b // 4 == layer, pltpu.roll(both, (4 * layer + 2) % 128, 1), packed)
+            low = pltpu.roll(both, (8 * layer + 2) % 128, 1)
+            high = pltpu.roll(both, (8 * layer + 5) % 128, 1)
+            packed = jnp.where(lane_b // 8 == layer, jnp.where(lane_b % 8 < 3, low, high), packed)
         e_send[rows, :] = packed
 
     halos = []
@@ -201,11 +210,8 @@
         rows = pl.ds(pl.multiple_of(8 + b * 16, 8), 16)
         for field in (init_x, mid_x):
             for layer in (0, NL + 1):
-                field[layer, rows, :] = jnp.zeros((16, BC + 128), F32)
-
-    @pl.loop(0, br // 16)
-    def _(b):
-        fwd[0, pl.ds(pl.multiple_of(b * 16, 16), 16), :] = jnp.zeros((16, BC), F32)
+                for c in range(2):
+                    field[layer, c, rows, :] = jnp.zeros((16, 128), F32)
 
     for halo in halos:
         halo.wait()
@@ -228,53 +234,98 @@
             noise_x[layer, TOP - 8:TOP, :] = pltpu.roll(rown[0, q], (6 - 2 * i) % 8, 0)
             noise_x[layer, end:end + 8, :] = pltpu.roll(rown[1, q], (-2 * i) % 8, 0)
 
+    groups = (br + 16) // 8
     lane8 = lax.broadcasted_iota(jnp.int32, (8, 128), 1)
-
-    @pl.loop(0, (br + 16) // 8)
+    place8 = lane8 % 8
+
+    def beside(packed):
+        return jnp.where(place8 == 3, pltpu.roll(packed, 126, 1), pltpu.roll(packed, 3, 1))
+
+    @pl.loop(0, groups)
     def _(b):
         rows = pl.ds(pl.multiple_of(8 + b * 8, 8), 8)
-        keep = jnp.where(b == 0, keep_top, jnp.where(b == (br + 16) // 8 - 1, keep_end, 1.0))
-        inverse = jnp.where(lane8 % 4 < 2, e_recv[0, rows, :] * (keep * keep_left), e_recv[1, rows, :] * (keep * keep_right))
+        own = pl.ds(pl.multiple_of(lax.min(lax.max(b - 1, 0), br // 8 - 1) * 8, 8), 8)
+        keep = jnp.where(b == 0, keep_top, jnp.where(b == groups - 1, keep_end, 1.0))
+        outer = jnp.where(place8 < 2, e_recv[0, rows, :] * (keep * keep_left), e_recv[1, rows, :] * (keep * keep_right))
+        inverse = jnp.where((place8 >= 2) & (place8 < 5), e_send[own, :], outer)
+        first = inverse * qn[rows, :]
         qi[rows, :] = inverse
-        qp[rows, :] = inverse * qn[rows, :]
-
-    def sideways(field):
-        return pltpu.roll(field, 1, 1) + pltpu.roll(field, BC + 127, 1)
-
-    def around(field, layer, first):
-        near = field[layer + 1, pl.ds(first - 8, 32), :]
-        rows = pl.ds(first, 16)
-        return near[7:23] + near[9:25] + sideways(near[8:24]) + field[layer, rows, :] + field[layer + 2, rows, :]
+        qp[rows, :] = first
+        h_init[rows, :] = beside(first)
+
+    @pl.loop(0, br // 8)
+    def _(b):
+        first = pl.multiple_of(TOP + b * 8, 8)
+        rows = pl.ds(first, 8)
+        here = qp[rows, :]
+        total = qp[pl.ds(first - 1, 8), :] + qp[pl.ds(first + 1, 8), :]
+        total = total + pltpu.roll(here, 1, 1) + pltpu.roll(here, 127, 1)
+        total = total + jnp.where(lane8 < 8, 0.0, pltpu.roll(here, 8, 1))
+        total = total + jnp.where(lane8 >= 120, 0.0, pltpu.roll(here, 120, 1))
+        h_mid[rows, :] = beside(qi[rows, :] * (qn[rows, :] + total))
+
+    lane_l = lane8 == 0
+    lane_r = lane8 == 127
+
+    def sums(field, layer, turn, halo, first):
+        rows = pl.ds(first, 8)
+        outer = pltpu.roll(halo[rows, :], turn, 1)
+        here = [field[layer + 1, c, rows, :] for c in range(2)]
+        back = [pltpu.roll(x, 1, 1) for x in here]
+        fore = [pltpu.roll(x, 127, 1) for x in here]
+        side = [
+            jnp.where(lane_l, outer, back[0]) + jnp.where(lane_r, fore[1], fore[0]),
+            jnp.where(lane_l, back[0], back[1]) + jnp.where(lane_r, outer, fore[1]),
+        ]
+        return [
+            side[c] + (field[layer + 1, c, pl.ds(first - 1, 8), :] + field[layer + 1, c, pl.ds(first + 1, 8), :])
+            + (field[layer, c, rows, :] + field[layer + 2, c, rows, :])
+            for c in range(2)
+        ]
 
     def initial(layer):
-        turn = lax.rem(254 - 4 * layer, 128)
-
-        @pl.loop(0, (br + 16) // 16)
+        @pl.loop(0, groups // UG)
         def _(b):
-            rows = pl.ds(pl.multiple_of(8 + b * 16, 8), 16)
-            init_x[layer + 1, rows, :BC] = inv_x[layer, rows, :] * noise_x[layer, rows, :]
-            init_x[layer + 1, rows, BC:] = pltpu.roll(qp[rows, :], turn, 1)
+            for g in range(UG):
+                rows = pl.ds(pl.multiple_of(8 + (b * UG + g) * 8, 8), 8)
+                for c in range(2):
+                    cols = slice(c * 128, c * 128 + 128)
+                    init_x[layer + 1, c, rows, :] = inv_x[layer, rows, cols] * noise_x[layer, rows, cols]
 
     def middle(layer):
-        turn = lax.rem(254 - 4 * layer, 128)
-
-        @pl.loop(0, (br + 16) // 16)
+        turn = lax.rem(252 - 8 * layer, 128)
+
+        @pl.loop(0, groups // UG)
         def _(b):
-            first = pl.multiple_of(8 + b * 16, 8)
-            rows = pl.ds(first, 16)
-            total = around(init_x, layer, first)
-            mid_x[layer + 1, rows, :BC] = inv_x[layer, rows, :] * (noise_x[layer, rows, :] + total[:, :BC])
-            mid_x[layer + 1, rows, BC:] = pltpu.roll(qi[rows, :], turn, 1) * (pltpu.roll(qn[rows, :], turn, 1) + total[:, BC:])
+            for g in range(UG):
+                first = pl.multiple_of(8 + (b * UG + g) * 8, 8)
+                rows = pl.ds(first, 8)
+                total = sums(init_x, layer, turn, h_init, first)
+                for c in range(2):
+                    cols = slice(c * 128, c * 128 + 128)
+                    mid_x[layer + 1, c, rows, :] = inv_x[layer, rows, cols] * (noise_x[layer, rows, cols] + total[c])
 
     def smooth(layer):
-        @pl.loop(0, br // 16)
+        turn = lax.rem(252 - 8 * layer, 128)
+        before = lax.max(layer - 1, 0)
+        keep = jnp.where(layer == 0, 0.0, 1.0).astype(F32)
+
+        @pl.loop(0, br // 8 // US)
         def _(b):
-            first = pl.multiple_of(TOP + b * 16, 16)
-            rows = pl.ds(first, 16)
-            own = pl.ds(pl.multiple_of(b * 16, 16), 16)
-            total = around(mid_x, layer, first)[:, :BC]
-            field = inv_x[layer, rows, :] * (noise_x[layer, rows, :] + total)
-            fwd[layer + 1, own, :] = (field + fwd[layer, own, :]) * kap[layer, own, :]
+            for g in range(US):
+                own = pl.multiple_of((b * US + g) * 8, 8)
+                first = pl.multiple_of(TOP + own, 8)
+                rows = pl.ds(first, 8)
+                total = sums(mid_x, layer, turn, h_mid, first)
+                for c in range(2):
+                    cols = slice(c * 128, c * 128 + 128)
+                    field = inv_x[layer, rows, cols] * (noise_x[layer, rows, cols] + total[c])
+                    previous = fwd[before, pl.ds(own, 8), cols] * keep
+                    fwd[layer, pl.ds(own, 8), cols] = (field + previous) * kap[layer, pl.ds(own, 8), cols]
+
+    @pl.loop(0, br // 8)
+    def _(b):
+        fwd[0, pl.ds(pl.multiple_of(b * 8, 8), 8), :] = jnp.zeros((8, BC), F32)
 
     @pl.loop(0, NL + 2)
     def _(step):
@@ -291,19 +342,6 @@
         def _():
             smooth(step - 2)
 
-    def result(b):
-        rows = pl.ds(pl.multiple_of(b * rb, rb), rb)
-        return pltpu.make_async_copy(fwd.at[1:NL + 1, rows, :], out.at[:, rows, :], out_sem.at[b])
-
-    @pl.loop(0, br // rb)
-    def _(b):
-        rows = pl.ds(pl.multiple_of(b * rb, rb), rb)
-        solved = fwd[NL, rows, :]
-        for layer in range(NL - 2, -1, -1):
-            solved = fwd[layer + 1, rows, :] + kap[layer, rows, :] * solved
-            fwd[layer + 1, rows, :] = solved
-        result(b).start()
-
     @pl.loop(0, NL)
     def _(layer):
         wait_bytes(noise.at[layer, :, :(nd - 1) * BC], bulk_send.at[layer])
@@ -315,9 +353,14 @@
         wait_bytes(rows_send, r_ssem)
         wait_bytes(q_send.at[:, 0:8, :], qh_ssem)
 
-    @pl.loop(0, br // rb)
-    def _(b):
-        result(b).wait()
+
+def back_kernel(fwd, pivots, out):
+    rows = pl.ds(pl.multiple_of(pl.program_id(0) * RB, RB), RB)
+    solved = fwd[NL - 1, rows, :]
+    out[NL - 1] = solved
+    for layer in range(NL - 2, -1, -1):
+        solved = fwd[layer, rows, :] + pivots[layer, rows, :] * solved
+        out[layer] = solved
 
 
 def body(noise, kappa, mask):
@@ -327,18 +370,18 @@
     dma = pltpu.SemaphoreType.DMA
     scratch = [
         pltpu.VMEM((NL, SR, nd * BC), F32),
-        pltpu.VMEM((NL, br, BC), F32),
         pltpu.VMEM((br, BC), jnp.int32),
         pltpu.VMEM((NL, ext, BC), F32),
         pltpu.VMEM((NL, ext, BC), F32),
-        pltpu.VMEM((NL + 2, ext, BC + 128), F32),
-        pltpu.VMEM((NL + 2, ext, BC + 128), F32),
-        pltpu.VMEM((NL + 1, br, BC), F32),
+        pltpu.VMEM((NL + 2, 2, ext, 128), F32),
+        pltpu.VMEM((NL + 2, 2, ext, 128), F32),
         pltpu.VMEM((NL // 4, 8, nd * BC), F32),
         pltpu.VMEM((2, NL // 4, 8, BC), F32),
         pltpu.VMEM((2, NL // 4, 8, BC), F32),
         pltpu.VMEM((2, NL // 4, 8, BC), F32),
         pltpu.VMEM((nd, SR, 128), F32),
+        pltpu.VMEM((ext, 128), F32),
+        pltpu.VMEM((ext, 128), F32),
         pltpu.VMEM((ext, 128), F32),
         pltpu.VMEM((ext, 128), F32),
         pltpu.VMEM((ext, 128), F32),
@@ -351,17 +394,26 @@
         dma((2,)), dma((2,)),
         dma((2,)), dma((2,)),
         dma((2, 2)), dma((2, 2)),
-        dma((br // 32,)),
     ]
-    return pl.pallas_call(
+    field = pltpu.VMEM((NL, br, BC), F32)
+    forward, pivots = pl.pallas_call(
         functools.partial(kernel, na, nd),
-        out_shape=jax.ShapeDtypeStruct((NL, br, BC), F32),
-        in_specs=[pl.BlockSpec(memory_space=pl.ANY)] * 3,
-        out_specs=pl.BlockSpec(memory_space=pl.ANY),
+        out_shape=(field, field),
+        in_specs=[pl.BlockSpec(memory_space=pltpu.HBM)] * 3,
+        out_specs=[pl.BlockSpec(memory_space=pltpu.VMEM)] * 2,
         scratch_shapes=scratch,
-        compiler_params=pltpu.CompilerParams(collective_id=0, has_side_effects=True, vmem_limit_bytes=60 << 20),
+        compiler_params=pltpu.CompilerParams(collective_id=0, has_side_effects=True, vmem_limit_bytes=48 << 20),
         name="sweeps",
     )(noise, kappa, mask)
+    return pl.pallas_call(
+        back_kernel,
+        grid=(br // RB,),
+        out_shape=jax.ShapeDtypeStruct((NL, br, BC), F32),
+        in_specs=[pl.BlockSpec(memory_space=pltpu.VMEM)] * 2,
+        out_specs=pl.BlockSpec((NL, RB, BC), lambda b: (0, b, 0)),
+        compiler_params=pltpu.CompilerParams(vmem_limit_bytes=16 << 20),
+        name="back",
+    )(forward, pivots)
 
 
 def solution(mesh):

time: 115 us -> 68.3 us (0.59)
  the two profiles are of different devices: /device:TPU:24 before, /device:TPU:1 now
where the time goes in v2:
time: 68.3 us; the launch traced here: 68.2 us
  Pallas kernels  68.2 us (100%)
    pallas_call x1, Pallas kernels, body(): pl.pallas_call(functools.partial(kernel, na, nd), out_shape=(field, field...  64.6 us
    pallas_call x1, Pallas kernels, body(): pl.pallas_call(back_kernel, grid=(br // RB,), out_shape=jax.ShapeDtypeStr...  3.58 us

profile of v2, /device:TPU:1, one launch (start us, length us, event | category | flops | bytes accessed | tf_op | source)
XLA Modules:
  0.0 68.2 jit_solution(11470068565337192167)
XLA Ops:
  0.0 64.6 %sweeps.1 = (f32[16,256,256]{2,1,0:T(8,128)S(1)}, f32[16,256,256]{2,1,0:T(8,128)S(1)}) custom-call(f32[16,16,4096]{2,1,0:T(8,128)} %noise.1, f32[16,256,256]{2,1,0:T(8,128)} %kappa.1, s32[256,256]{1,0:T(8,128)} %mask.1), custom_call_target="tpu_custom_call" | custom-call | tf_op jit(solution)/shard_map/sweeps/pallas_call | solution.py:399
  64.6 3.6 %back.1 = f32[16,256,256]{2,1,0:T(8,128)} custom-call(f32[16,256,256]{2,1,0:T(8,128)S(1)} %get-tuple-element.7.fwd, f32[16,256,256]{2,1,0:T(8,128)S(1)} %get-tuple-element.8.pivots), custom_call_target="tpu_custom_call" | custom-call | tf_op jit(solution)/shard_map/back/pallas_call | solution.py:408

commit v3 on v2

v3 whole, which is shorter than its diff:
```python
import functools

import jax
import jax.numpy as jnp
from jax import lax
from jax.experimental import pallas as pl
from jax.experimental.pallas import tpu as pltpu
from jax.sharding import PartitionSpec as P

MESH = pl.DeviceIdType.MESH
F32 = jnp.float32
NL = 16
SR = 16
BC = 256
TOP = 16
LAG = 2
RB = 32
EARLY = 4


def wait_bytes(ref, sem):
    pltpu.make_async_copy(ref, ref, sem).wait()


def kernel(na, nd, noise, kappa, mask, fwd, kap, *scratch):
    (strip, msk, noise_x, inv_x, init_x, mid_x, mid_h, rows_send, rowi_send, rown, rowi, q_send, q_recv, qn, qp,
     h_init, h_mid, h_inv, e_send, f_send, f_recv, c_recv, load_sem, bulk_send, bulk_recv, q_ssem, q_rsem, r_ssem, r_rsem, qh_ssem, qh_rsem,
     e_ssem, e_rsem, i_ssem, i_rsem, c_ssem, c_rsem) = scratch
    br = nd * SR
    end = TOP + br
    a, d = lax.axis_index("ax"), lax.axis_index("ay")
    above, below = lax.rem(a + na - 1, na), lax.rem(a + 1, na)
    left, right = lax.rem(d + nd - 1, nd), lax.rem(d + 1, nd)

    loads = [
        pltpu.make_async_copy(noise, strip, load_sem.at[0]),
        pltpu.make_async_copy(kappa, kap, load_sem.at[1]),
        pltpu.make_async_copy(mask, msk, load_sem.at[2]),
    ]
    for load in loads:
        load.start()

    barrier = pltpu.get_barrier_semaphore()

    def greet(x, y):
        pl.semaphore_signal(barrier, inc=1, device_id=(x, y), device_id_type=MESH)

    @pl.loop(1, nd)
    def _(k):
        greet(a, lax.rem(d + k, nd))

    for x in (above, below):
        for y in (d, left, right):
            greet(x, y)
    greet(above, nd - 1)
    greet(below, 0)
    edge = jnp.where(d == 0, nd, 0) + jnp.where(d == nd - 1, nd, 0)
    pl.semaphore_wait(barrier, nd - 1 + 6 + edge)

    def bulk(layer):
        pltpu.make_async_copy(
            noise.at[layer, :, pl.ds(pl.multiple_of(d * BC, BC), BC)],
            noise_x.at[layer, pl.ds(pl.multiple_of(TOP + d * SR, SR), SR), :],
            bulk_recv.at[layer],
        ).start()

        @pl.loop(1, nd)
        def _(k):
            t = lax.rem(d + k, nd)
            pltpu.make_async_remote_copy(
                src_ref=noise.at[layer, :, pl.ds(pl.multiple_of(t * BC, BC), BC)],
                dst_ref=noise_x.at[layer, pl.ds(pl.multiple_of(TOP + d * SR, SR), SR), :],
                send_sem=bulk_send.at[layer],
                recv_sem=bulk_recv.at[layer],
                device_id=(a, t),
                device_id_type=MESH,
            ).start()

    @pl.loop(0, EARLY)
    def _(layer):
        bulk(layer)

    lane = lax.broadcasted_iota(jnp.int32, (8, 128), 1)
    sub = lax.broadcasted_iota(jnp.int32, (8, BC), 0)

    loads[0].wait()

    @pl.loop(0, nd)
    def _(t):
        before = pl.multiple_of(lax.rem(t + nd - 1, nd) * BC + 128, 128)
        after = pl.multiple_of(lax.rem(t + 1, nd) * BC, 128)
        packed = jnp.zeros((8, 128), F32)
        for layer in range(NL):
            for half in range(2):
                rows = slice(half * 8, half * 8 + 8)
                both = jnp.where(lane < 64, strip[layer, rows, pl.ds(after, 128)], strip[layer, rows, pl.ds(before, 128)])
                packed = jnp.where(lane // 4 == layer + 16 * half, pltpu.roll(both, (4 * layer + 2 + 64 * half) % 128, 1), packed)
        q_send[t] = packed

    def q_place(s):
        return q_recv.at[s + 1]

    pltpu.make_async_copy(q_send.at[d], q_place(d), q_rsem).start()

    @pl.loop(1, nd)
    def _(k):
        t = lax.rem(d + k, nd)
        pltpu.make_async_remote_copy(
            src_ref=q_send.at[t], dst_ref=q_place(d), send_sem=q_ssem, recv_sem=q_rsem,
            device_id=(a, t), device_id_type=MESH,
        ).start()

    def pick_rows(tile, first, i):
        return pltpu.roll(tile, (2 * i - first) % 8, 0)

    def send_rows(first_row, first, x, slot):
        @pl.loop(0, nd)
        def _(t):
            cols = pl.ds(pl.multiple_of(t * BC, BC), BC)
            for q in range(NL // 4):
                packed = jnp.zeros((8, BC), F32)
                for i in range(4):
                    tile = strip[4 * q + i, first_row:first_row + 8, cols]
                    packed = jnp.where(sub // 2 == i, pick_rows(tile, first, i), packed)
                rows_send[q, :, cols] = packed
            pltpu.make_async_remote_copy(
                src_ref=rows_send.at[:, :, cols], dst_ref=rown.at[slot], send_sem=r_ssem, recv_sem=r_rsem.at[slot],
                device_id=(x, t), device_id_type=MESH,
            ).start()
            pltpu.make_async_remote_copy(
                src_ref=q_send.at[t], dst_ref=q_recv.at[(0, nd + 1)[slot]], send_sem=qh_ssem,
                recv_sem=qh_rsem.at[slot], device_id=(x, t), device_id_type=MESH,
            ).start()

    @pl.when(d == 0)
    def _():
        send_rows(0, 0, above, 1)

    @pl.when(d == nd - 1)
    def _():
        send_rows(SR - 8, 6, below, 0)

    loads[1].wait()
    loads[2].wait()
    rb = 32
    lane_b = lax.broadcasted_iota(jnp.int32, (rb, 128), 1)

    @pl.loop(0, br // rb)
    def _(b):
        rows = pl.ds(pl.multiple_of(b * rb, rb), rb)
        active = msk[rows, :].astype(F32)
        packed = jnp.zeros((rb, 128), F32)
        for layer in range(NL):
            inverse = active / (6.0 + kap[layer, rows, :])
            inv_x[layer, pl.ds(pl.multiple_of(TOP + b * rb, 16), rb), :] = inverse
            both = jnp.where(lane_b < 64, inverse[:, :128], inverse[:, 128:])
            packed = jnp.where(lane_b // 4 == layer, pltpu.roll(both, (4 * layer + 2) % 128, 1), packed)
        e_send[rows, :] = packed

    folds = ((0, 2, 64, 66), (0, 126, 64, 62))
    fr = br // 4
    place = lane % 4

    @pl.loop(0, fr // 8)
    def _(b):
        for slot in range(2):
            packed = jnp.zeros((8, 128), F32)
            for k in range(4):
                piece = pltpu.roll(e_send[pl.ds(pl.multiple_of(k * fr + b * 8, 8), 8), :], folds[slot][k], 1)
                low = (0, 2, 0, 2)[k] if slot == 0 else (2, 0, 2, 0)[k]
                mine = (place >= low) & (place < low + 2) & (lane // 64 == k // 2)
                packed = jnp.where(mine, piece, packed)
            f_send[slot, pl.ds(pl.multiple_of(b * 8, 8), 8), :] = packed

    halos = []
    for slot, y in ((0, right), (1, left)):
        halos.append(pltpu.make_async_remote_copy(
            src_ref=f_send.at[slot], dst_ref=f_recv.at[slot], send_sem=e_ssem.at[slot], recv_sem=e_rsem.at[slot],
            device_id=(a, y), device_id_type=MESH,
        ))
        halos.append(pltpu.make_async_remote_copy(
            src_ref=e_send.at[br - 8:br, :], dst_ref=c_recv.at[slot, 0], send_sem=c_ssem.at[slot, 0],
            recv_sem=c_rsem.at[slot, 0], device_id=(below, y), device_id_type=MESH,
        ))
        halos.append(pltpu.make_async_remote_copy(
            src_ref=e_send.at[0:8, :], dst_ref=c_recv.at[slot, 1], send_sem=c_ssem.at[slot, 1],
            recv_sem=c_rsem.at[slot, 1], device_id=(above, y), device_id_type=MESH,
        ))
    for q in range(NL // 4):
        down = jnp.zeros((8, BC), F32)
        up = jnp.zeros((8, BC), F32)
        for i in range(4):
            layer = 4 * q + i
            down = jnp.where(sub // 2 == i, pick_rows(inv_x[layer, end - 8:end, :], 6, i), down)
            up = jnp.where(sub // 2 == i, pick_rows(inv_x[layer, TOP:TOP + 8, :], 0, i), up)
        rowi_send[0, q] = down
        rowi_send[1, q] = up
    for slot, x in ((0, below), (1, above)):
        halos.append(pltpu.make_async_remote_copy(
            src_ref=rowi_send.at[slot], dst_ref=rowi.at[slot], send_sem=i_ssem.at[slot], recv_sem=i_rsem.at[slot],
            device_id=(x, d), device_id_type=MESH,
        ))
    for halo in halos:
        halo.start()

    @pl.loop(EARLY, NL)
    def _(layer):
        bulk(layer)

    @pl.loop(0, br // rb)
    def _(b):
        rows = pl.ds(pl.multiple_of(b * rb, rb), rb)
        pivot = jnp.zeros((rb, BC), F32)
        for layer in range(NL):
            pivot = 1.0 / (2.5 + kap[layer, rows, :] - pivot)
            kap[layer, rows, :] = pivot

    @pl.loop(0, (br + 16) // 16)
    def _(b):
        rows = pl.ds(pl.multiple_of(8 + b * 16, 8), 16)
        for field in (init_x, mid_x):
            for layer in (0, NL + 1):
                for c in range(2):
                    field[layer, c, rows, :] = jnp.zeros((16, 128), F32)

    for halo in halos:
        halo.wait()
    for slot in range(2):
        wait_bytes(rown.at[slot], r_rsem.at[slot])
        wait_bytes(q_recv.at[slot], qh_rsem.at[slot])
    wait_bytes(q_recv.at[1:nd + 1], q_rsem)
    keep_top = jnp.where(a > 0, 1.0, 0.0).astype(F32)
    keep_end = jnp.where(a < na - 1, 1.0, 0.0).astype(F32)
    keep_left = jnp.where(d > 0, 1.0, 0.0).astype(F32)
    keep_right = jnp.where(d < nd - 1, 1.0, 0.0).astype(F32)

    @pl.loop(0, NL // 4)
    def _(q):
        for i in range(4):
            layer = 4 * q + i
            inv_x[layer, TOP - 8:TOP, :] = keep_top * pltpu.roll(rowi[0, q], (6 - 2 * i) % 8, 0)
            inv_x[layer, end:end + 8, :] = keep_end * pltpu.roll(rowi[1, q], (-2 * i) % 8, 0)
            noise_x[layer, TOP - 8:TOP, :] = pltpu.roll(rown[0, q], (6 - 2 * i) % 8, 0)
            noise_x[layer, end:end + 8, :] = pltpu.roll(rown[1, q], (-2 * i) % 8, 0)

    groups = (br + 16) // 8

    def beside(packed):
        return jnp.where(place == 1, pltpu.roll(packed, 127, 1), pltpu.roll(packed, 1, 1))

    def sides(first, from_left, from_right, noise_q):
        rows = pl.ds(first, 8)
        inverse = jnp.where(place < 2, from_left * keep_left, from_right * keep_right)
        qn[rows, :] = noise_q
        qp[rows, :] = inverse * noise_q
        h_inv[rows, :] = inverse

    sides(TOP - 8, c_recv[0, 0] * keep_top, c_recv[1, 0] * keep_top, pltpu.roll(q_recv[0], 64, 1))
    sides(end, c_recv[0, 1] * keep_end, c_recv[1, 1] * keep_end, q_recv[nd + 1])
    for k in range(4):
        @pl.loop(0, fr // SR)
        def _(b):
            noise_q = q_recv[1 + k * (fr // SR) + b]
            for half in range(2):
                rows = pl.ds(pl.multiple_of(b * SR + half * 8, 8), 8)
                pieces = [pltpu.roll(f_recv[slot, rows, :], (128 - folds[slot][k]) % 128, 1) for slot in range(2)]
                first = pl.multiple_of(TOP + k * fr + b * SR + half * 8, 8)
                sides(first, *pieces, pltpu.roll(noise_q, 64, 1) if half else noise_q)

    @pl.loop(0, br // 8)
    def _(b):
        first = pl.multiple_of(TOP + b * 8, 8)
        rows = pl.ds(first, 8)
        here = qp[rows, :]
        total = qp[pl.ds(first - 1, 8), :] + qp[pl.ds(first + 1, 8), :]
        total = total + jnp.where(place < 2, pltpu.roll(here, 1, 1), pltpu.roll(here, 127, 1))
        total = total + jnp.where(lane < 4, 0.0, pltpu.roll(here, 4, 1))
        total = total + jnp.where(lane >= 60, 0.0, pltpu.roll(here, 124, 1))
        inverse = h_inv[rows, :]
        h_mid[rows, :] = beside(inverse * (qn[rows, :] + total))
        h_inv[rows, :] = beside(inverse)

    @pl.loop(0, groups)
    def _(b):
        rows = pl.ds(pl.multiple_of(8 + b * 8, 8), 8)
        h_init[rows, :] = beside(qp[rows, :])

    @pl.loop(0, br // 8)
    def _(b):
        fwd[0, pl.ds(pl.multiple_of(b * 8, 8), 8), :] = jnp.zeros((8, BC), F32)

    lane_l = lane == 0
    lane_r = lane == 127
    cols = (slice(0, 128), slice(128, 256))

    def around(field, layer, first, here, outer):
        rows = pl.ds(first, 8)
        back = [pltpu.roll(x, 1, 1) for x in here]
        fore = [pltpu.roll(x, 127, 1) for x in here]
        side = (
            jnp.where(lane_l, outer, back[0]) + jnp.where(lane_r, fore[1], fore[0]),
            jnp.where(lane_l, back[0], back[1]) + jnp.where(lane_r, outer, fore[1]),
        )
        return [
            side[c] + (field[layer + 1, c, pl.ds(first - 1, 8), :] + field[layer + 1, c, pl.ds(first + 1, 8), :])
            + field[layer, c, rows, :]
            for c in range(2)
        ]

    def group(step, first, do_initial, do_middle, do_smooth):
        rows = pl.ds(first, 8)
        stores = []
        initial = middle = None
        if do_initial:
            initial = [inv_x[step, rows, cols[c]] * noise_x[step, rows, cols[c]] for c in range(2)]
            stores += [(init_x, (step + 1, c, rows, slice(None)), initial[c]) for c in range(2)]
        if do_middle:
            layer = step - 1
            turn = lax.rem(254 - 4 * layer, 128)
            here = [init_x[layer + 1, c, rows, :] for c in range(2)]
            total = around(init_x, layer, first, here, pltpu.roll(h_init[rows, :], turn, 1))
            if initial is not None:
                total = [total[c] + initial[c] for c in range(2)]
            middle = [inv_x[layer, rows, cols[c]] * (noise_x[layer, rows, cols[c]] + total[c]) for c in range(2)]
            inner = jnp.where(lane < 64, here[0], here[1])
            outer = pltpu.roll(h_mid[rows, :], turn, 1) + pltpu.roll(h_inv[rows, :], turn, 1) * inner
            stores += [(mid_x, (layer + 1, c, rows, slice(None)), middle[c]) for c in range(2)]
            stores += [(mid_h, (layer, rows, slice(None)), outer)]
        if do_smooth:
            layer = step - 2
            own = pl.ds(pl.multiple_of(first - TOP, 8), 8)
            here = [mid_x[layer + 1, c, rows, :] for c in range(2)]
            total = around(mid_x, layer, first, here, mid_h[layer, rows, :])
            if middle is not None:
                total = [total[c] + middle[c] for c in range(2)]
            for c in range(2):
                field = inv_x[layer, rows, cols[c]] * (noise_x[layer, rows, cols[c]] + total[c])
                previous = fwd[lax.max(layer - 1, 0), own, cols[c]]
                pivot = kap[layer, own, cols[c]]
                stores += [(fwd, (layer, own, cols[c]), (field + previous) * pivot)]
        return stores

    def sweep(step, do_initial, do_middle, do_smooth):
        pending = []
        low, high = (0, groups) if do_middle else (1, groups - 1)
        for g in range(low, high):
            pending.append(group(step, 8 + 8 * g, do_initial, do_middle, do_smooth and 1 <= g < groups - 1))
            if len(pending) > LAG:
                for ref, index, value in pending.pop(0):
                    ref[index] = value
        for stores in pending:
            for ref, index, value in stores:
                ref[index] = value

    for step in range(2):
        wait_bytes(noise_x.at[step, TOP:end, :], bulk_recv.at[step])

        @pl.loop(0, groups)
        def _(b):
            for ref, index, value in group(step, pl.multiple_of(8 + b * 8, 8), True, step > 0, False):
                ref[index] = value

    @pl.loop(2, NL)
    def _(step):
        wait_bytes(noise_x.at[step, TOP:end, :], bulk_recv.at[step])
        sweep(step, True, True, True)

    sweep(NL, False, True, True)
    sweep(NL + 1, False, False, True)

    @pl.loop(0, NL)
    def _(layer):
        wait_bytes(noise.at[layer, :, :(nd - 1) * BC], bulk_send.at[layer])

    wait_bytes(q_send.at[:nd - 1], q_ssem)

    @pl.when((d == 0) | (d == nd - 1))
    def _():
        wait_bytes(rows_send, r_ssem)
        wait_bytes(q_send, qh_ssem)


def back_kernel(fwd, pivots, out, solution_x, out_sem):
    def result(b):
        rows = pl.ds(pl.multiple_of(b * RB, RB), RB)
        return pltpu.make_async_copy(solution_x.at[:, rows, :], out.at[:, rows, :], out_sem.at[b])

    steps = fwd.shape[1] // RB

    @pl.loop(0, steps)
    def _(b):
        rows = pl.ds(pl.multiple_of(b * RB, RB), RB)
        solved = fwd[NL - 1, rows, :]
        solution_x[NL - 1, rows, :] = solved
        for layer in range(NL - 2, -1, -1):
            solved = fwd[layer, rows, :] + pivots[layer, rows, :] * solved
            solution_x[layer, rows, :] = solved
        result(b).start()

    @pl.loop(0, steps)
    def _(b):
        result(b).wait()


def body(noise, kappa, mask):
    na, nd = lax.axis_size("ax"), lax.axis_size("ay")
    br = nd * SR
    ext = br + 2 * TOP
    dma = pltpu.SemaphoreType.DMA
    scratch = [
        pltpu.VMEM((NL, SR, nd * BC), F32),
        pltpu.VMEM((br, BC), jnp.int32),
        pltpu.VMEM((NL, ext, BC), F32),
        pltpu.VMEM((NL, ext, BC), F32),
        pltpu.VMEM((NL + 2, 2, ext, 128), F32),
        pltpu.VMEM((NL + 2, 2, ext, 128), F32),
        pltpu.VMEM((NL, ext, 128), F32),
        pltpu.VMEM((NL // 4, 8, nd * BC), F32),
        pltpu.VMEM((2, NL // 4, 8, BC), F32),
        pltpu.VMEM((2, NL // 4, 8, BC), F32),
        pltpu.VMEM((2, NL // 4, 8, BC), F32),
        pltpu.VMEM((nd, 8, 128), F32),
        pltpu.VMEM((nd + 2, 8, 128), F32),
        pltpu.VMEM((ext, 128), F32),
        pltpu.VMEM((ext, 128), F32),
        pltpu.VMEM((ext, 128), F32),
        pltpu.VMEM((ext, 128), F32),
        pltpu.VMEM((ext, 128), F32),
        pltpu.VMEM((br, 128), F32),
        pltpu.VMEM((2, br // 4, 128), F32),
        pltpu.VMEM((2, br // 4, 128), F32),
        pltpu.VMEM((2, 2, 8, 128), F32),
        dma((3,)), dma((NL,)), dma((NL,)),
        dma, dma,
        dma, dma((2,)),
        dma, dma((2,)),
        dma((2,)), dma((2,)),
        dma((2,)), dma((2,)),
        dma((2, 2)), dma((2, 2)),
    ]
    field = pltpu.VMEM((NL, br, BC), F32)
    forward, pivots = pl.pallas_call(
        functools.partial(kernel, na, nd),
        out_shape=(field, field),
        in_specs=[pl.BlockSpec(memory_space=pltpu.HBM)] * 3,
        out_specs=[pl.BlockSpec(memory_space=pltpu.VMEM)] * 2,
        scratch_shapes=scratch,
        compiler_params=pltpu.CompilerParams(collective_id=0, has_side_effects=True, vmem_limit_bytes=48 << 20),
        name="sweeps",
    )(noise, kappa, mask)
    return pl.pallas_call(
        back_kernel,
        out_shape=jax.ShapeDtypeStruct((NL, br, BC), F32),
        in_specs=[pl.BlockSpec(memory_space=pltpu.VMEM)] * 2,
        out_specs=pl.BlockSpec(memory_space=pltpu.HBM),
        scratch_shapes=[field, dma((br // RB,))],
        compiler_params=pltpu.CompilerParams(vmem_limit_bytes=16 << 20),
        name="back",
    )(forward, pivots)


def solution(mesh):
    in_specs = (P(None, ("ax", "ay"), None), P(None, "ax", "ay"), P("ax", "ay"))
    out_specs = P(None, "ax", "ay")
    return jax.shard_map(body, mesh=mesh, in_specs=in_specs, out_specs=out_specs, check_vma=False)
```

time: 68.3 us -> 63.6 us (0.931)
  Pallas kernels: 68.2 us -> 63.5 us
    pallas_call x1, Pallas kernels: 64.6 us -> 61.4 us  [body(): pl.pallas_call(functools.partial(kernel, na, nd), out_shape=(field, field...]
    pallas_call x1, Pallas kernels: 3.58 us -> 2.12 us  [body(): pl.pallas_call(back_kernel, out_shape=jax.ShapeDtypeStruct((NL, br, BC),...]
where the time goes in v3:
time: 63.6 us; the launch traced here: 63.5 us
  Pallas kernels  63.5 us (100%)
    pallas_call x1, Pallas kernels, body(): pl.pallas_call(functools.partial(kernel, na, nd), out_shape=(field, field...  61.4 us
    pallas_call x1, Pallas kernels, body(): pl.pallas_call(back_kernel, out_shape=jax.ShapeDtypeStruct((NL, br, BC),...  2.12 us

profile of v3, /device:TPU:1, one launch (start us, length us, event | category | flops | bytes accessed | tf_op | source)
XLA Modules:
  0.0 63.5 jit_solution(16247852705796277903)
XLA Ops:
  0.0 61.4 %sweeps.1 = (f32[16,256,256]{2,1,0:T(8,128)S(1)}, f32[16,256,256]{2,1,0:T(8,128)S(1)}) custom-call(f32[16,16,4096]{2,1,0:T(8,128)} %noise.1, f32[16,256,256]{2,1,0:T(8,128)} %kappa.1, s32[256,256]{1,0:T(8,128)} %mask.1), custom_call_target="tpu_custom_call" | custom-call | tf_op jit(solution)/shard_map/sweeps/pallas_call | solution.py:442
  61.4 2.1 %back.1 = f32[16,256,256]{2,1,0:T(8,128)} custom-call(f32[16,256,256]{2,1,0:T(8,128)S(1)} %get-tuple-element.7.fwd, f32[16,256,256]{2,1,0:T(8,128)S(1)} %get-tuple-element.8.pivots), custom_call_target="tpu_custom_call" | custom-call | tf_op jit(solution)/shard_map/back/pallas_call | solution.py:451

commit v4 on v3

--- a/solution.py
+++ b/solution.py
@@ -49,13 +49,31 @@
     def _(k):
         greet(a, lax.rem(d + k, nd))
 
-    for x in (above, below):
-        for y in (d, left, right):
-            greet(x, y)
-    greet(above, nd - 1)
-    greet(below, 0)
     edge = jnp.where(d == 0, nd, 0) + jnp.where(d == nd - 1, nd, 0)
-    pl.semaphore_wait(barrier, nd - 1 + 6 + edge)
+    odd = lax.rem(a, 2)
+
+    @pl.when(odd == 0)
+    def _():
+        @pl.loop(0, nd)
+        def _(k):
+            greet(above, lax.rem(d + k, nd))
+            greet(below, lax.rem(d + k, nd))
+
+    pl.semaphore_wait(barrier, nd - 1 + odd * (2 * nd))
+
+    @pl.when(odd == 1)
+    def _():
+        for x in (above, below):
+            for y in (d, left, right):
+                greet(x, y)
+        greet(above, nd - 1)
+        greet(below, 0)
+        for y, x in ((0, above), (nd - 1, below)):
+            @pl.when(d == y)
+            def _():
+                @pl.loop(0, nd)
+                def _(t):
+                    greet(x, t)
 
     def bulk(layer):
         pltpu.make_async_copy(
@@ -70,7 +88,7 @@
             pltpu.make_async_remote_copy(
                 src_ref=noise.at[layer, :, pl.ds(pl.multiple_of(t * BC, BC), BC)],
                 dst_ref=noise_x.at[layer, pl.ds(pl.multiple_of(TOP + d * SR, SR), SR), :],
-                send_sem=bulk_send.at[layer],
+                send_sem=bulk_send,
                 recv_sem=bulk_recv.at[layer],
                 device_id=(a, t),
                 device_id_type=MESH,
@@ -131,6 +149,10 @@
                 src_ref=q_send.at[t], dst_ref=q_recv.at[(0, nd + 1)[slot]], send_sem=qh_ssem,
                 recv_sem=qh_rsem.at[slot], device_id=(x, t), device_id_type=MESH,
             ).start()
+
+    @pl.when(odd == 0)
+    def _():
+        pl.semaphore_wait(barrier, 8 + edge)
 
     @pl.when(d == 0)
     def _():
@@ -368,9 +390,7 @@
     sweep(NL, False, True, True)
     sweep(NL + 1, False, False, True)
 
-    @pl.loop(0, NL)
-    def _(layer):
-        wait_bytes(noise.at[layer, :, :(nd - 1) * BC], bulk_send.at[layer])
+    wait_bytes(noise.at[:, :, :(nd - 1) * BC], bulk_send)
 
     wait_bytes(q_send.at[:nd - 1], q_ssem)
 
@@ -430,7 +450,7 @@
         pltpu.VMEM((2, br // 4, 128), F32),
         pltpu.VMEM((2, br // 4, 128), F32),
         pltpu.VMEM((2, 2, 8, 128), F32),
-        dma((3,)), dma((NL,)), dma((NL,)),
+        dma((3,)), dma, dma((NL,)),
         dma, dma,
         dma, dma((2,)),
         dma, dma((2,)),

time: 63.6 us -> 61.5 us (0.967)
  Pallas kernels: 63.5 us -> 61.2 us
    pallas_call x1, Pallas kernels: 61.4 us -> 59 us  [body(): pl.pallas_call(functools.partial(kernel, na, nd), out_shape=(field, field...]
where the time goes in v4:
time: 61.5 us; the launch traced here: 61.2 us
  Pallas kernels  61.2 us (100%)
    pallas_call x1, Pallas kernels, body(): pl.pallas_call(functools.partial(kernel, na, nd), out_shape=(field, field...  59 us
    pallas_call x1, Pallas kernels, body(): pl.pallas_call(back_kernel, out_shape=jax.ShapeDtypeStruct((NL, br, BC),...  2.12 us

profile of v4, /device:TPU:1, one launch (start us, length us, event | category | flops | bytes accessed | tf_op | source)
XLA Modules:
  0.0 61.2 jit_solution(5494262608047766485)
XLA Ops:
  0.0 59.0 %sweeps.1 = (f32[16,256,256]{2,1,0:T(8,128)S(1)}, f32[16,256,256]{2,1,0:T(8,128)S(1)}) custom-call(f32[16,16,4096]{2,1,0:T(8,128)} %noise.1, f32[16,256,256]{2,1,0:T(8,128)} %kappa.1, s32[256,256]{1,0:T(8,128)} %mask.1), custom_call_target="tpu_custom_call" | custom-call | tf_op jit(solution)/shard_map/sweeps/pallas_call | solution.py:462
  59.0 2.1 %back.1 = f32[16,256,256]{2,1,0:T(8,128)} custom-call(f32[16,256,256]{2,1,0:T(8,128)S(1)} %get-tuple-element.7.fwd, f32[16,256,256]{2,1,0:T(8,128)S(1)} %get-tuple-element.8.pivots), custom_call_target="tpu_custom_call" | custom-call | tf_op jit(solution)/shard_map/back/pallas_call | solution.py:471

commit v5 on v4

--- a/solution.py
+++ b/solution.py
@@ -15,6 +15,7 @@
 TOP = 16
 LAG = 2
 RB = 32
+COLS = (slice(0, 128), slice(128, 256))
 EARLY = 4
 
 
@@ -22,10 +23,67 @@
     pltpu.make_async_copy(ref, ref, sem).wait()
 
 
-def kernel(na, nd, noise, kappa, mask, fwd, kap, *scratch):
-    (strip, msk, noise_x, inv_x, init_x, mid_x, mid_h, rows_send, rowi_send, rown, rowi, q_send, q_recv, qn, qp,
-     h_init, h_mid, h_inv, e_send, f_send, f_recv, c_recv, load_sem, bulk_send, bulk_recv, q_ssem, q_rsem, r_ssem, r_rsem, qh_ssem, qh_rsem,
-     e_ssem, e_rsem, i_ssem, i_rsem, c_ssem, c_rsem) = scratch
+def around(field, layer, first, here, outer):
+    rows = pl.ds(first, 8)
+    lane = lax.broadcasted_iota(jnp.int32, (8, 128), 1)
+    lane_l, lane_r = lane == 0, lane == 127
+    back = [pltpu.roll(x, 1, 1) for x in here]
+    fore = [pltpu.roll(x, 127, 1) for x in here]
+    side = (
+        jnp.where(lane_l, outer, back[0]) + jnp.where(lane_r, fore[1], fore[0]),
+        jnp.where(lane_l, back[0], back[1]) + jnp.where(lane_r, outer, fore[1]),
+    )
+    return [
+        side[c] + (field[layer + 1, c, pl.ds(first - 1, 8), :] + field[layer + 1, c, pl.ds(first + 1, 8), :])
+        + field[layer, c, rows, :]
+        for c in range(2)
+    ]
+
+def group(refs, step, first, do_initial, do_middle, do_smooth):
+    fwd, kap, noise_x, inv_x, init_x, mid_x, mid_h, h_init, h_mid, h_inv = refs
+    rows = pl.ds(first, 8)
+    lane = lax.broadcasted_iota(jnp.int32, (8, 128), 1)
+    stores = []
+    initial = middle = None
+    if do_initial:
+        initial = [inv_x[step, rows, COLS[c]] * noise_x[step, rows, COLS[c]] for c in range(2)]
+        stores += [(init_x, (step + 1, c, rows, slice(None)), initial[c]) for c in range(2)]
+    if do_middle:
+        layer = step - 1
+        turn = lax.rem(254 - 4 * layer, 128)
+        here = [init_x[layer + 1, c, rows, :] for c in range(2)]
+        total = around(init_x, layer, first, here, pltpu.roll(h_init[rows, :], turn, 1))
+        if initial is not None:
+            total = [total[c] + initial[c] for c in range(2)]
+        middle = [inv_x[layer, rows, COLS[c]] * (noise_x[layer, rows, COLS[c]] + total[c]) for c in range(2)]
+        inner = jnp.where(lane < 64, here[0], here[1])
+        outer = pltpu.roll(h_mid[rows, :], turn, 1) + pltpu.roll(h_inv[rows, :], turn, 1) * inner
+        stores += [(mid_x, (layer + 1, c, rows, slice(None)), middle[c]) for c in range(2)]
+        stores += [(mid_h, (layer, rows, slice(None)), outer)]
+    if do_smooth:
+        layer = step - 2
+        own = pl.ds(pl.multiple_of(first - TOP, 8), 8)
+        here = [mid_x[layer + 1, c, rows, :] for c in range(2)]
+        total = around(mid_x, layer, first, here, mid_h[layer, rows, :])
+        if middle is not None:
+            total = [total[c] + middle[c] for c in range(2)]
+        for c in range(2):
+            field = inv_x[layer, rows, COLS[c]] * (noise_x[layer, rows, COLS[c]] + total[c])
+            previous = fwd[lax.max(layer - 1, 0), own, COLS[c]]
+            pivot = kap[layer, own, COLS[c]]
+            stores += [(fwd, (layer, own, COLS[c]), (field + previous) * pivot)]
+    return stores
+
+
+def put(stores):
+    for ref, index, value in stores:
+        ref[index] = value
+
+
+def kernel(na, nd, noise, kappa, mask, *refs):
+    fwd, kap, noise_x, inv_x, init_x, mid_x, mid_h, h_init, h_mid, h_inv = refs[:10]
+    (strip, msk, rows_send, rowi_send, rown, rowi, q_send, q_recv, qn, qp, e_send, f_send, f_recv, c_recv, load_sem, bulk_send, bulk_recv, q_ssem, q_rsem, r_ssem, r_rsem, qh_ssem, qh_rsem,
+     e_ssem, e_rsem, i_ssem, i_rsem, c_ssem, c_rsem) = refs[10:]
     br = nd * SR
     end = TOP + br
     a, d = lax.axis_index("ax"), lax.axis_index("ay")
@@ -311,84 +369,29 @@
     def _(b):
         fwd[0, pl.ds(pl.multiple_of(b * 8, 8), 8), :] = jnp.zeros((8, BC), F32)
 
-    lane_l = lane == 0
-    lane_r = lane == 127
-    cols = (slice(0, 128), slice(128, 256))
-
-    def around(field, layer, first, here, outer):
-        rows = pl.ds(first, 8)
-        back = [pltpu.roll(x, 1, 1) for x in here]
-        fore = [pltpu.roll(x, 127, 1) for x in here]
-        side = (
-            jnp.where(lane_l, outer, back[0]) + jnp.where(lane_r, fore[1], fore[0]),
-            jnp.where(lane_l, back[0], back[1]) + jnp.where(lane_r, outer, fore[1]),
-        )
-        return [
-            side[c] + (field[layer + 1, c, pl.ds(first - 1, 8), :] + field[layer + 1, c, pl.ds(first + 1, 8), :])
-            + field[layer, c, rows, :]
-            for c in range(2)
-        ]
-
-    def group(step, first, do_initial, do_middle, do_smooth):
-        rows = pl.ds(first, 8)
-        stores = []
-        initial = middle = None
-        if do_initial:
-            initial = [inv_x[step, rows, cols[c]] * noise_x[step, rows, cols[c]] for c in range(2)]
-            stores += [(init_x, (step + 1, c, rows, slice(None)), initial[c]) for c in range(2)]
-        if do_middle:
-            layer = step - 1
-            turn = lax.rem(254 - 4 * layer, 128)
-            here = [init_x[layer + 1, c, rows, :] for c in range(2)]
-            total = around(init_x, layer, first, here, pltpu.roll(h_init[rows, :], turn, 1))
-            if initial is not None:
-                total = [total[c] + initial[c] for c in range(2)]
-            middle = [inv_x[layer, rows, cols[c]] * (noise_x[layer, rows, cols[c]] + total[c]) for c in range(2)]
-            inner = jnp.where(lane < 64, here[0], here[1])
-            outer = pltpu.roll(h_mid[rows, :], turn, 1) + pltpu.roll(h_inv[rows, :], turn, 1) * inner
-            stores += [(mid_x, (layer + 1, c, rows, slice(None)), middle[c]) for c in range(2)]
-            stores += [(mid_h, (layer, rows, slice(None)), outer)]
-        if do_smooth:
-            layer = step - 2
-            own = pl.ds(pl.multiple_of(first - TOP, 8), 8)
-            here = [mid_x[layer + 1, c, rows, :] for c in range(2)]
-            total = around(mid_x, layer, first, here, mid_h[layer, rows, :])
-            if middle is not None:
-                total = [total[c] + middle[c] for c in range(2)]
-            for c in range(2):
-                field = inv_x[layer, rows, cols[c]] * (noise_x[layer, rows, cols[c]] + total[c])
-                previous = fwd[lax.max(layer - 1, 0), own, cols[c]]
-                pivot = kap[layer, own, cols[c]]
-                stores += [(fwd, (layer, own, cols[c]), (field + previous) * pivot)]
-        return stores
-
     def sweep(step, do_initial, do_middle, do_smooth):
         pending = []
         low, high = (0, groups) if do_middle else (1, groups - 1)
         for g in range(low, high):
-            pending.append(group(step, 8 + 8 * g, do_initial, do_middle, do_smooth and 1 <= g < groups - 1))
+            pending.append(group(refs[:10], step, 8 + 8 * g, do_initial, do_middle, do_smooth and 1 <= g < groups - 1))
             if len(pending) > LAG:
-                for ref, index, value in pending.pop(0):
-                    ref[index] = value
+                put(pending.pop(0))
         for stores in pending:
-            for ref, index, value in stores:
-                ref[index] = value
+            put(stores)
 
     for step in range(2):
         wait_bytes(noise_x.at[step, TOP:end, :], bulk_recv.at[step])
 
         @pl.loop(0, groups)
         def _(b):
-            for ref, index, value in group(step, pl.multiple_of(8 + b * 8, 8), True, step > 0, False):
-                ref[index] = value
-
-    @pl.loop(2, NL)
+            put(group(refs[:10], step, pl.multiple_of(8 + b * 8, 8), True, step > 0, False))
+
+    @pl.loop(2, NL - 1)
     def _(step):
         wait_bytes(noise_x.at[step, TOP:end, :], bulk_recv.at[step])
         sweep(step, True, True, True)
 
-    sweep(NL, False, True, True)
-    sweep(NL + 1, False, False, True)
+    wait_bytes(noise_x.at[NL - 1, TOP:end, :], bulk_recv.at[NL - 1])
 
     wait_bytes(noise.at[:, :, :(nd - 1) * BC], bulk_send)
 
@@ -400,25 +403,46 @@
         wait_bytes(q_send, qh_ssem)
 
 
-def back_kernel(fwd, pivots, out, solution_x, out_sem):
+def back_kernel(*refs):
+    fwd, kap = refs[:2]
+    out, solution_x, out_sem = refs[10:]
+    size = RB // 8
+    steps = fwd.shape[1] // RB
+
     def result(b):
-        rows = pl.ds(pl.multiple_of(b * RB, RB), RB)
+        rows = pl.ds(b * RB, RB)
         return pltpu.make_async_copy(solution_x.at[:, rows, :], out.at[:, rows, :], out_sem.at[b])
 
-    steps = fwd.shape[1] // RB
-
-    @pl.loop(0, steps)
-    def _(b):
-        rows = pl.ds(pl.multiple_of(b * RB, RB), RB)
-        solved = fwd[NL - 1, rows, :]
-        solution_x[NL - 1, rows, :] = solved
-        for layer in range(NL - 2, -1, -1):
-            solved = fwd[layer, rows, :] + pivots[layer, rows, :] * solved
-            solution_x[layer, rows, :] = solved
-        result(b).start()
-
-    @pl.loop(0, steps)
-    def _(b):
+    def sweep_group(step, g, do_initial, do_middle):
+        inside = 0 < g < last
+        if not 0 <= g <= last or not (inside or do_middle):
+            return []
+        return group(refs[:10], step, 8 + 8 * g, do_initial, do_middle, inside)
+
+    def back(g):
+        rows = pl.ds(8 * g - 8, 8)
+        for c in COLS:
+            solved = fwd[NL - 1, rows, c]
+            solution_x[NL - 1, rows, c] = solved
+            for layer in range(NL - 2, -1, -1):
+                solved = fwd[layer, rows, c] + kap[layer, rows, c] * solved
+                solution_x[layer, rows, c] = solved
+
+    last = steps * size + 1
+    pending = []
+    for turn in range(last + 10):
+        pending.append([])
+        if len(pending) > LAG:
+            put(pending.pop(0))
+        for lag, stage in ((0, (NL - 1, True, True)), (3, (NL, False, True)), (6, (NL + 1, False, False))):
+            pending[-1] += sweep_group(stage[0], turn - lag, *stage[1:])
+        g = turn - 9
+        if 0 < g < last:
+            back(g)
+            if g % size == 0:
+                result(g // size - 1).start()
+
+    for b in range(steps):
         result(b).wait()
 
 
@@ -430,20 +454,12 @@
     scratch = [
         pltpu.VMEM((NL, SR, nd * BC), F32),
         pltpu.VMEM((br, BC), jnp.int32),
-        pltpu.VMEM((NL, ext, BC), F32),
-        pltpu.VMEM((NL, ext, BC), F32),
-        pltpu.VMEM((NL + 2, 2, ext, 128), F32),
-        pltpu.VMEM((NL + 2, 2, ext, 128), F32),
-        pltpu.VMEM((NL, ext, 128), F32),
         pltpu.VMEM((NL // 4, 8, nd * BC), F32),
         pltpu.VMEM((2, NL // 4, 8, BC), F32),
         pltpu.VMEM((2, NL // 4, 8, BC), F32),
         pltpu.VMEM((2, NL // 4, 8, BC), F32),
         pltpu.VMEM((nd, 8, 128), F32),
         pltpu.VMEM((nd + 2, 8, 128), F32),
-        pltpu.VMEM((ext, 128), F32),
-        pltpu.VMEM((ext, 128), F32),
-        pltpu.VMEM((ext, 128), F32),
         pltpu.VMEM((ext, 128), F32),
         pltpu.VMEM((ext, 128), F32),
         pltpu.VMEM((br, 128), F32),
@@ -459,24 +475,35 @@
         dma((2, 2)), dma((2, 2)),
     ]
     field = pltpu.VMEM((NL, br, BC), F32)
-    forward, pivots = pl.pallas_call(
+    fields = (
+        field, field,
+        pltpu.VMEM((NL, ext, BC), F32),
+        pltpu.VMEM((NL, ext, BC), F32),
+        pltpu.VMEM((NL + 2, 2, ext, 128), F32),
+        pltpu.VMEM((NL + 2, 2, ext, 128), F32),
+        pltpu.VMEM((NL, ext, 128), F32),
+        pltpu.VMEM((ext, 128), F32),
+        pltpu.VMEM((ext, 128), F32),
+        pltpu.VMEM((ext, 128), F32),
+    )
+    fields = pl.pallas_call(
         functools.partial(kernel, na, nd),
-        out_shape=(field, field),
+        out_shape=fields,
         in_specs=[pl.BlockSpec(memory_space=pltpu.HBM)] * 3,
-        out_specs=[pl.BlockSpec(memory_space=pltpu.VMEM)] * 2,
+        out_specs=[pl.BlockSpec(memory_space=pltpu.VMEM)] * 10,
         scratch_shapes=scratch,
-        compiler_params=pltpu.CompilerParams(collective_id=0, has_side_effects=True, vmem_limit_bytes=48 << 20),
+        compiler_params=pltpu.CompilerParams(collective_id=0, has_side_effects=True, vmem_limit_bytes=16 << 20),
         name="sweeps",
-    )(noise, kappa, mask)
+    )(*(pltpu.with_memory_space_constraint(x, pltpu.HBM) for x in (noise, kappa, mask)))
     return pl.pallas_call(
         back_kernel,
         out_shape=jax.ShapeDtypeStruct((NL, br, BC), F32),
-        in_specs=[pl.BlockSpec(memory_space=pltpu.VMEM)] * 2,
+        in_specs=[pl.BlockSpec(memory_space=pltpu.VMEM)] * 10,
         out_specs=pl.BlockSpec(memory_space=pltpu.HBM),
         scratch_shapes=[field, dma((br // RB,))],
         compiler_params=pltpu.CompilerParams(vmem_limit_bytes=16 << 20),
         name="back",
-    )(forward, pivots)
+    )(*fields)
 
 
 def solution(mesh):

time: 61.5 us -> 60.8 us (0.989)
  Pallas kernels: 61.2 us -> 60.4 us
    pallas_call x1, Pallas kernels: 59 us -> 58 us  [body(): pl.pallas_call(functools.partial(kernel, na, nd), out_shape=fields, in_sp...]
where the time goes in v5:
time: 60.8 us; the launch traced here: 60.4 us
  Pallas kernels  60.4 us (99%)
    pallas_call x1, Pallas kernels, body(): pl.pallas_call(functools.partial(kernel, na, nd), out_shape=fields, in_sp...  58 us
    pallas_call x1, Pallas kernels, body(): pl.pallas_call(back_kernel, out_shape=jax.ShapeDtypeStruct((NL, br, BC),...  2.43 us

profile of v5, /device:TPU:1, one launch (start us, length us, event | category | flops | bytes accessed | tf_op | source)
XLA Modules:
  0.0 60.4 jit_solution(13717166360585997478)
XLA Ops:
  0.0 58.0 %sweeps.1 = (f32[16,256,256]{2,1,0:T(8,128)S(1)}, f32[16,256,256]{2,1,0:T(8,128)S(1)}, f32[16,288,256]{2,1,0:T(8,128)S(1)}, f32[16,288,256]{2,1,0:T(8,128)S(1)},...) custom-call(f32[16,16,4096]{2,1,0:T(8,128)} %noise.1, ...), custom_call_target="tpu_custom_call" | custom-call | tf_op jit(solution)/shard_map/sweeps/pallas_call | solution.py:489
  58.0 2.4 %back.1 = f32[16,256,256]{2,1,0:T(8,128)} custom-call(f32[16,256,256]{2,1,0:T(8,128)S(1)} %get-tuple-element.15.refs_0_, f32[16,256,256]{2,1,0:T(8,128)S(1)} %get-tuple-element.16.refs_1_, f32[16,288,256]{2,1,0:T(8,128)S(1)} %get-tuple-element.17.refs_2_, f32[16,288,256]{2,1,0:T(8,128)S(1)} %get-tuple-element.18.refs_3_, ...), custom_call_target="tpu_custom_call" | custom-call | tf_op jit(solution)/shard_map/back/pallas_call | solution.py:498

commit v6 on v5

--- a/solution.py
+++ b/solution.py
@@ -14,7 +14,7 @@
 BC = 256
 TOP = 16
 LAG = 2
-RB = 32
+WB = 16
 COLS = (slice(0, 128), slice(128, 256))
 EARLY = 4
 
@@ -406,11 +406,11 @@
 def back_kernel(*refs):
     fwd, kap = refs[:2]
     out, solution_x, out_sem = refs[10:]
-    size = RB // 8
-    steps = fwd.shape[1] // RB
+    size = WB // 8
+    steps = fwd.shape[1] // WB
 
     def result(b):
-        rows = pl.ds(b * RB, RB)
+        rows = pl.ds(b * WB, WB)
         return pltpu.make_async_copy(solution_x.at[:, rows, :], out.at[:, rows, :], out_sem.at[b])
 
     def sweep_group(step, g, do_initial, do_middle):
@@ -430,13 +430,13 @@
 
     last = steps * size + 1
     pending = []
-    for turn in range(last + 10):
+    for turn in range(last + 7):
         pending.append([])
-        if len(pending) > LAG:
+        if len(pending) > 1:
             put(pending.pop(0))
-        for lag, stage in ((0, (NL - 1, True, True)), (3, (NL, False, True)), (6, (NL + 1, False, False))):
+        for lag, stage in ((0, (NL - 1, True, True)), (2, (NL, False, True)), (4, (NL + 1, False, False))):
             pending[-1] += sweep_group(stage[0], turn - lag, *stage[1:])
-        g = turn - 9
+        g = turn - 6
         if 0 < g < last:
             back(g)
             if g % size == 0:
@@ -500,7 +500,7 @@
         out_shape=jax.ShapeDtypeStruct((NL, br, BC), F32),
         in_specs=[pl.BlockSpec(memory_space=pltpu.VMEM)] * 10,
         out_specs=pl.BlockSpec(memory_space=pltpu.HBM),
-        scratch_shapes=[field, dma((br // RB,))],
+        scratch_shapes=[field, dma((br // WB,))],
         compiler_params=pltpu.CompilerParams(vmem_limit_bytes=16 << 20),
         name="back",
     )(*fields)

time: 60.8 us -> 60.8 us (level)
  no operation moved by 1% of the time
where the time goes in v6:
time: 60.8 us; the launch traced here: 60.4 us
  Pallas kernels  60.4 us (99%)
    pallas_call x1, Pallas kernels, body(): pl.pallas_call(functools.partial(kernel, na, nd), out_shape=fields, in_sp...  58 us
    pallas_call x1, Pallas kernels, body(): pl.pallas_call(back_kernel, out_shape=jax.ShapeDtypeStruct((NL, br, BC),...  2.4 us

profile of v6, /device:TPU:1, one launch (start us, length us, event | category | flops | bytes accessed | tf_op | source)
XLA Modules:
  0.0 60.4 jit_solution(6411721621031283056)
XLA Ops:
  0.0 58.0 %sweeps.1 = (f32[16,256,256]{2,1,0:T(8,128)S(1)}, f32[16,256,256]{2,1,0:T(8,128)S(1)}, f32[16,288,256]{2,1,0:T(8,128)S(1)}, f32[16,288,256]{2,1,0:T(8,128)S(1)},...) custom-call(f32[16,16,4096]{2,1,0:T(8,128)} %noise.1, ...), custom_call_target="tpu_custom_call" | custom-call | tf_op jit(solution)/shard_map/sweeps/pallas_call | solution.py:489
  58.0 2.4 %back.1 = f32[16,256,256]{2,1,0:T(8,128)} custom-call(f32[16,256,256]{2,1,0:T(8,128)S(1)} %get-tuple-element.15.refs_0_, f32[16,256,256]{2,1,0:T(8,128)S(1)} %get-tuple-element.16.refs_1_, f32[16,288,256]{2,1,0:T(8,128)S(1)} %get-tuple-element.17.refs_2_, f32[16,288,256]{2,1,0:T(8,128)S(1)} %get-tuple-element.18.refs_3_, ...), custom_call_target="tpu_custom_call" | custom-call | tf_op jit(solution)/shard_map/back/pallas_call | solution.py:498

commit v7 on v5

--- a/solution.py
+++ b/solution.py
@@ -103,8 +103,7 @@
     def greet(x, y):
         pl.semaphore_signal(barrier, inc=1, device_id=(x, y), device_id_type=MESH)
 
-    @pl.loop(1, nd)
-    def _(k):
+    for k in range(1, nd):
         greet(a, lax.rem(d + k, nd))
 
     edge = jnp.where(d == 0, nd, 0) + jnp.where(d == nd - 1, nd, 0)
@@ -112,8 +111,7 @@
 
     @pl.when(odd == 0)
     def _():
-        @pl.loop(0, nd)
-        def _(k):
+        for k in range(nd):
             greet(above, lax.rem(d + k, nd))
             greet(below, lax.rem(d + k, nd))
 
@@ -140,8 +138,7 @@
             bulk_recv.at[layer],
         ).start()
 
-        @pl.loop(1, nd)
-        def _(k):
+        for k in range(1, nd):
             t = lax.rem(d + k, nd)
             pltpu.make_async_remote_copy(
                 src_ref=noise.at[layer, :, pl.ds(pl.multiple_of(t * BC, BC), BC)],

time: 60.8 us -> 60.6 us (level)
  no operation moved by 1% of the time
where the time goes in v7:
time: 60.6 us; the launch traced here: 60.4 us
  Pallas kernels  60.4 us (100%)
    pallas_call x1, Pallas kernels, body(): pl.pallas_call(functools.partial(kernel, na, nd), out_shape=fields, in_sp...  58 us
    pallas_call x1, Pallas kernels, body(): pl.pallas_call(back_kernel, out_shape=jax.ShapeDtypeStruct((NL, br, BC),...  2.43 us

profile of v7, /device:TPU:1, one launch (start us, length us, event | category | flops | bytes accessed | tf_op | source)
XLA Modules:
  0.0 60.4 jit_solution(7577365360042974626)
XLA Ops:
  0.0 58.0 %sweeps.1 = (f32[16,256,256]{2,1,0:T(8,128)S(1)}, f32[16,256,256]{2,1,0:T(8,128)S(1)}, f32[16,288,256]{2,1,0:T(8,128)S(1)}, f32[16,288,256]{2,1,0:T(8,128)S(1)},...) custom-call(f32[16,16,4096]{2,1,0:T(8,128)} %noise.1, ...), custom_call_target="tpu_custom_call" | custom-call | tf_op jit(solution)/shard_map/sweeps/pallas_call | solution.py:486
  58.0 2.4 %back.1 = f32[16,256,256]{2,1,0:T(8,128)} custom-call(f32[16,256,256]{2,1,0:T(8,128)S(1)} %get-tuple-element.15.refs_0_, f32[16,256,256]{2,1,0:T(8,128)S(1)} %get-tuple-element.16.refs_1_, f32[16,288,256]{2,1,0:T(8,128)S(1)} %get-tuple-element.17.refs_2_, f32[16,288,256]{2,1,0:T(8,128)S(1)} %get-tuple-element.18.refs_3_, ...), custom_call_target="tpu_custom_call" | custom-call | tf_op jit(solution)/shard_map/back/pallas_call | solution.py:495
